TPU v7x, 32 devices: a whole 2x2x4 slice. The times are simulated.
32 devices in a mesh: fsdp: 4 (over x, core), replica: 8 (over z, y).
Axes of the slice: x: 2, y: 2, z: 4, core: 2. Of those that a mesh axis runs over, the one named last changes fastest.
Arguments:
- weights: float32 [32, 512, 2048], P('replica', 'fsdp'), may hold values from -0.125 to 0.125
- momentum: bfloat16 [32, 512, 2048], P('replica', 'fsdp'), may hold values from -6 to 6
- tokens: bfloat16 [28672, 2048], P(('fsdp', 'replica')), may hold values from -6 to 6
- block_expert: int32 [224], P(('fsdp', 'replica')), may hold values from 0 to 31, as said below
- owner_expert: int32 [32], replicated, may hold values from 0 to 31, as said below
Outputs:
- fresh: bfloat16 [32, 512, 2048], P(('fsdp', 'replica'))
- rollout: bfloat16 [28672, 512], P(('fsdp', 'replica'))
Inputs may be any that keep to these rules, and one draw needn't show every extreme that they name: `owner_expert`: within each group g the entries g * N to g * N + N - 1 (N the fsdp axis size) are a permutation of the expert numbers g * N to g * N + N - 1. `block_expert`: the blocks of the device at fsdp index f and replica index r are blocks (f * R + r) * 7 to (f * R + r) * 7 + 7 - 1 (R the replica axis size). Each names an expert that owner_expert assigns to fsdp index f; the 7 blocks of one device name experts of distinct groups; in every fsdp index one group is named by every device of that index.
All inputs are finite; a program needn't handle non-finite values.
Results may differ from a plain program's by a relative error of at most 0.008.
Values may be sent and summed in bfloat16 or wider, within the bound.
No kernel may reach another device: no remote copies, remote signals or barrier semaphores. Data moves between devices by JAX's collectives and lax.ppermute only.
A program may use at most 128 MiB of HBM per device.

v0:
```python
import math

import jax
import jax.numpy as jnp
from jax import lax
from jax.sharding import PartitionSpec as P

ROWS_E = 512
COLS = 2048
ITERS = 4


quintic_one = 3.4445
quintic_two = -4.775
quintic_three = 2.0315
learn_rate = 0.05
weight_decay = 0.1
norm_eps = 1e-07


def orthogonalize(moment):
    wide = moment.astype(jnp.float32)
    state = (wide / (jnp.sqrt(jnp.sum(wide * wide)) + norm_eps)).astype(jnp.bfloat16)
    for _ in range(ITERS):
        square = lax.dot_general(
            state, state, (((1,), (1,)), ((), ())), preferred_element_type=jnp.float32
        ).astype(jnp.bfloat16)
        twice = jnp.dot(square, square, preferred_element_type=jnp.float32)
        poly = (quintic_two * square.astype(jnp.float32) + quintic_three * twice).astype(
            jnp.bfloat16
        )
        state = (
            quintic_one * state.astype(jnp.float32)
            + jnp.dot(poly, state, preferred_element_type=jnp.float32)
        ).astype(jnp.bfloat16)
    return state


def finish(master, update):
    factor = learn_rate * 0.2 * math.sqrt(max(ROWS_E, COLS))
    return (
        master * (1.0 - learn_rate * weight_decay) - factor * update.astype(jnp.float32)
    ).astype(jnp.bfloat16)


def per_device(weights, momentum, tokens, block_expert, owner_expert):
    owners = lax.axis_size("fsdp")
    groups = lax.axis_size("replica")
    group = lax.axis_index("replica")
    table = lax.dynamic_slice_in_dim(owner_expert, group * owners, owners, 0)
    local = table - group * owners
    sent_moment = jnp.take(momentum, local, axis=0)
    sent_master = jnp.take(weights, local, axis=0)
    whole_master, whole_moment = (
        lax.all_to_all(sent_master, "fsdp", split_axis=0, concat_axis=1, tiled=True),
        lax.all_to_all(
            sent_moment.astype(jnp.float32), "fsdp", split_axis=0, concat_axis=1, tiled=True
        ),
    )
    update = orthogonalize(whole_moment[0].astype(jnp.bfloat16))
    refreshed = finish(whole_master[0], update)
    fresh = refreshed[None]
    blocks = block_expert.shape[0]
    width = tokens.shape[1]
    resident = tokens.reshape(blocks, -1, width)
    target = block_expert // owners
    selector = (target[:, None] == jnp.arange(groups, dtype=jnp.int32)[None, :]).astype(
        jnp.bfloat16
    )
    outgoing = jnp.einsum(
        "bg,brd->grd", selector, resident, preferred_element_type=jnp.float32
    ).astype(jnp.bfloat16)
    product = jnp.einsum(
        "grd,od->gro",
        lax.all_to_all(outgoing, "replica", split_axis=0, concat_axis=0, tiled=True),
        refreshed,
        preferred_element_type=jnp.float32,
    ).astype(jnp.bfloat16)
    answers = lax.all_to_all(product, "replica", split_axis=0, concat_axis=0, tiled=True)
    picked = jnp.einsum(
        "bg,gro->bro", selector, answers, preferred_element_type=jnp.float32
    ).astype(jnp.bfloat16)
    rollout = picked.reshape(-1, answers.shape[2])
    return (fresh, rollout)


def solution(mesh):
    placed = (
        P("replica", "fsdp", None),
        P("replica", "fsdp", None),
        P(("fsdp", "replica"), None),
        P(("fsdp", "replica")),
        P(),
    )
    return jax.shard_map(
        per_device,
        mesh=mesh,
        in_specs=placed,
        out_specs=(P(("fsdp", "replica"), None, None), P(("fsdp", "replica"), None)),
        check_vma=False,
    )
```

profile of v0, /device:TPU:16, one launch (start us, length us, event | category | flops | bytes accessed | tf_op | source)
XLA Modules:
  0.0 225.4 jit_solution(10607689608692742643)
XLA Ops:
  2.2 2.0 gather_fusion.1
  4.2 3.2 %select_convert_fusion = bf16[4,128,2048]{2,1,0:T(8,128)(2,1)} fusion(bf16[4,128,2048]{2,1,0:T(8,128)(2,1)} %gather_fusion.1, pred[4]{0:T(512)(128)(4,1)S(1)} %get-tuple-element.2), kind=kLoop, calls=%fused_computation.18 | loop fusion | flops 1048576 | bytes 4194308 | tf_op jit(solution)/shard_map/convert_element_type | solution.py:57
  7.4 4.5 %all-to-all-start.1 = ((bf16[4,128,2048]{2,1,0:T(8,128)(2,1)}), bf16[4,128,2048]{2,1,0:T(8,128)(2,1)}, u32[]{:S(2)}, u32[]{:S(2)}) async-start(bf16[4,128,2048]{2,1,0:T(8,128)(2,1)} %select_convert_fusion), calls=%async_computation.1 | async-start | bytes 4194304 | tf_op jit(solution)/shard_map/all_to_all | solution.py:56
  11.9 5.0 %gather_fusion = f32[4,128,2048]{2,1,0:T(8,128)} fusion(f32[4,128,2048]{2,1,0:T(8,128)} %param.5, s32[1024]{0:T(1024)S(1)} %pad_clamp_fusion), kind=kCustom, calls=%fused_computation | custom fusion | bytes 8388624 | tf_op jit(solution)/shard_map/jit(_take)/gather | solution.py:53
  16.9 4.9 %broadcast_select_fusion = f32[4,128,2048]{2,1,0:T(8,128)} fusion(f32[4,128,2048]{2,1,0:T(8,128)} %gather_fusion, pred[4]{0:T(512)(128)(4,1)S(1)} %get-tuple-element.2), kind=kLoop, calls=%fused_computation.20 | loop fusion | flops 1048576 | bytes 8388612 | tf_op jit(solution)/shard_map/jit(_take)/select_n | solution.py:53
  21.8 15.9 %all-to-all-done.1 = bf16[4,128,2048]{2,1,0:T(8,128)(2,1)} async-done(((bf16[4,128,2048]{2,1,0:T(8,128)(2,1)}), bf16[4,128,2048]{2,1,0:T(8,128)(2,1)}, u32[]{:S(2)}, u32[]{:S(2)}) %all-to-all-start.1) | async-done | bytes 2097184 | tf_op jit(solution)/shard_map/all_to_all | solution.py:56
  37.7 4.9 %all-to-all-start = ((f32[4,128,2048]{2,1,0:T(8,128)}), f32[4,128,2048]{2,1,0:T(8,128)}, u32[]{:S(2)}, u32[]{:S(2)}) async-start(f32[4,128,2048]{2,1,0:T(8,128)} %broadcast_select_fusion), calls=%async_computation | async-start | bytes 8388608 | tf_op jit(solution)/shard_map/all_to_all | solution.py:55
  42.6 5.0 %fusion.7 = bf16[8,128,2048]{2,0,1:T(8,128)(2,1)S(1)} fusion(bf16[7,128,2048]{2,1,0:T(8,128)(2,1)} %bitcast.38, s32[7]{0:T(128)S(1)} %and_select_fusion), kind=kOutput, calls=%fused_computation.16 | convolution fusion | flops 31457336 | bytes 7864348 | tf_op jit(solution)/shard_map/bg,brd->grd/dot_general | solution.py:70
  47.6 4.2 %copy.15 = bf16[8,128,2048]{2,1,0:T(8,128)(2,1)} copy(bf16[8,128,2048]{2,0,1:T(8,128)(2,1)S(1)} %fusion.7) | data formatting | bytes 8388608 | tf_op jit(solution)/shard_map/convert_element_type | solution.py:72
  51.8 39.0 %all-to-all-done = f32[4,128,2048]{2,1,0:T(8,128)} async-done(((f32[4,128,2048]{2,1,0:T(8,128)}), f32[4,128,2048]{2,1,0:T(8,128)}, u32[]{:S(2)}, u32[]{:S(2)}) %all-to-all-start) | async-done | bytes 4194336 | tf_op jit(solution)/shard_map/all_to_all | solution.py:55
  90.8 6.2 %all-to-all-start.2 = ((bf16[8,128,2048]{2,1,0:T(8,128)(2,1)}), bf16[8,128,2048]{2,1,0:T(8,128)(2,1)}, u32[]{:S(2)}, u32[]{:S(2)}) async-start(bf16[8,128,2048]{2,1,0:T(8,128)(2,1)} %copy.15), calls=%async_computation.2 | async-start | bytes 8388608 | tf_op jit(solution)/shard_map/all_to_all | solution.py:75
  97.0 3.3 %fusion = f32[]{:T(128)} fusion(bf16[4,128,2048]{2,1,0:T(8,128)(2,1)} %all-to-all-done.1), kind=kLoop, calls=%fused_computation.4 | loop fusion | flops 3145727 | bytes 2097156 | tf_op jit(solution)/shard_map/reduce_sum | solution.py:23
  100.9 2.0 fusion.1
  105.6 5.1 %add_convert_fusion.3 = bf16[512,2048]{1,0:T(8,128)(2,1)} fusion(bf16[512,2048]{1,0:T(8,128)(2,1)} %bitcast.40, bf16[512,512]{1,0:T(8,128)(2,1)S(1)} %convolution_convert_fusion.4), kind=kOutput, calls=%fused_computation.15 | convolution fusion | flops 1347682304 | bytes 4718592 | tf_op jit(solution)/shard_map/dot_general | solution.py:34
  110.7 3.5 %convolution_convert_fusion.3 = bf16[512,512]{1,0:T(8,128)(2,1)S(1)} fusion(bf16[512,2048]{1,0:T(8,128)(2,1)} %add_convert_fusion.3), kind=kOutput, calls=%fused_computation.37 | convolution fusion | flops 1074003968 | bytes 2621440 | tf_op jit(solution)/shard_map/dot_general | solution.py:25
  114.2 5.1 %add_convert_fusion.2 = bf16[512,2048]{1,0:T(8,128)(2,1)} fusion(bf16[512,2048]{1,0:T(8,128)(2,1)} %add_convert_fusion.3, bf16[512,512]{1,0:T(8,128)(2,1)S(1)} %convolution_convert_fusion.3), kind=kOutput, calls=%fused_computation.14 | convolution fusion | flops 1347682304 | bytes 4718592 | tf_op jit(solution)/shard_map/dot_general | solution.py:34
  119.3 3.5 %convolution_convert_fusion.2 = bf16[512,512]{1,0:T(8,128)(2,1)S(1)} fusion(bf16[512,2048]{1,0:T(8,128)(2,1)} %add_convert_fusion.2), kind=kOutput, calls=%fused_computation.36 | convolution fusion | flops 1074003968 | bytes 2621440 | tf_op jit(solution)/shard_map/dot_general | solution.py:25
  122.8 5.1 %add_convert_fusion.1 = bf16[512,2048]{1,0:T(8,128)(2,1)} fusion(bf16[512,2048]{1,0:T(8,128)(2,1)} %add_convert_fusion.2, bf16[512,512]{1,0:T(8,128)(2,1)S(1)} %convolution_convert_fusion.2), kind=kOutput, calls=%fused_computation.13 | convolution fusion | flops 1347682304 | bytes 4718592 | tf_op jit(solution)/shard_map/dot_general | solution.py:34
  127.9 3.5 %convolution_convert_fusion.1 = bf16[512,512]{1,0:T(8,128)(2,1)S(1)} fusion(bf16[512,2048]{1,0:T(8,128)(2,1)} %add_convert_fusion.1), kind=kOutput, calls=%fused_computation.35 | convolution fusion | flops 1074003968 | bytes 2621440 | tf_op jit(solution)/shard_map/dot_general | solution.py:25
  131.5 4.9 %broadcast_multiply_fusion = f32[4,128,2048]{2,1,0:T(8,128)} fusion(f32[4,128,2048]{2,1,0:T(8,128)} %all-to-all-done), kind=kLoop, calls=%fused_computation.19 | loop fusion | flops 1048576 | bytes 8388608 | tf_op jit(solution)/shard_map/mul | solution.py:42
  136.3 6.5 %fusion.2 = bf16[512,2048]{1,0:T(8,128)(2,1)} fusion(f32[4,128,2048]{2,1,0:T(8,128)} %broadcast_multiply_fusion, bf16[512,2048]{1,0:T(8,128)(2,1)} %add_convert_fusion.1, bf16[512,512]{1,0:T(8,128)(2,1)S(1)} %convolution_convert_fusion.1), kind=kOutput, calls=%fused_computation.7 | convolution fusion | flops 1351876608 | bytes 8912896 | tf_op jit(solution)/shard_map/dot_general | solution.py:34
  142.9 43.8 %all-to-all-done.2 = bf16[8,128,2048]{2,1,0:T(8,128)(2,1)} async-done(((bf16[8,128,2048]{2,1,0:T(8,128)(2,1)}), bf16[8,128,2048]{2,1,0:T(8,128)(2,1)}, u32[]{:S(2)}, u32[]{:S(2)}) %all-to-all-start.2) | async-done | bytes 4194336 | tf_op jit(solution)/shard_map/all_to_all | solution.py:75
  186.7 5.5 %fusion.11 = bf16[8,128,512]{2,0,1:T(8,128)(2,1)S(1)} fusion(bf16[512,2048]{1,0:T(8,128)(2,1)} %fusion.2, bf16[8,128,2048]{2,1,0:T(8,128)(2,1)} %all-to-all-done.2), kind=kOutput, calls=%fused_computation.22 | convolution fusion | flops 2148007936 | bytes 7340032 | tf_op jit(solution)/shard_map/grd,od->gro/dot_general | solution.py:73
  192.5 30.9 %all_to_all.28 = bf16[8,128,512]{2,1,0:T(8,128)(2,1)S(1)} all-to-all(bf16[8,128,512]{2,1,0:T(8,128)(2,1)S(1)} %copy.17), channel_id=1, replica_groups=mesh['fsdp'=4,'replica'=8] {'replica'}, dimensions={0} | all-to-all | bytes 2097152 | tf_op jit(solution)/shard_map/all_to_all | solution.py:79
  (13 shorter events, 6.5 us)
Async XLA Ops:
  0.6 1.6 copy-start
  7.4 30.2 %all-to-all-start.1 = ((bf16[4,128,2048]{2,1,0:T(8,128)(2,1)}), bf16[4,128,2048]{2,1,0:T(8,128)(2,1)}, u32[]{:S(2)}, u32[]{:S(2)}) async-start(bf16[4,128,2048]{2,1,0:T(8,128)(2,1)} %select_convert_fusion), calls=%async_computation.1 | async-start | bytes 4194304 | tf_op jit(solution)/shard_map/all_to_all | solution.py:56
  21.8 20.8 %copy-start.2 = (s32[7]{0:T(128)S(1)}, s32[7]{0:T(128)}, u32[]{:S(2)}) copy-start(s32[7]{0:T(128)} %param.8) | copy-start | bytes 88
  37.7 53.2 %all-to-all-start = ((f32[4,128,2048]{2,1,0:T(8,128)}), f32[4,128,2048]{2,1,0:T(8,128)}, u32[]{:S(2)}, u32[]{:S(2)}) async-start(f32[4,128,2048]{2,1,0:T(8,128)} %broadcast_select_fusion), calls=%async_computation | async-start | bytes 8388608 | tf_op jit(solution)/shard_map/all_to_all | solution.py:55
  90.8 95.9 %all-to-all-start.2 = ((bf16[8,128,2048]{2,1,0:T(8,128)(2,1)}), bf16[8,128,2048]{2,1,0:T(8,128)(2,1)}, u32[]{:S(2)}, u32[]{:S(2)}) async-start(bf16[8,128,2048]{2,1,0:T(8,128)(2,1)} %copy.15), calls=%async_computation.2 | async-start | bytes 8388608 | tf_op jit(solution)/shard_map/all_to_all | solution.py:75
  103.0 1.3 copy-start.1
where the time goes:
time: 229 us; the launch traced here: 225 us
  waiting for transfers between devices  98.7 us (43%)
  matrix products  44.9 us (20%)
  blocking collectives  30.9 us (13%)
  other arithmetic  19.1 us (8%)
  starting transfers between devices  15.6 us (7%)
  local copies, waits for them, and re-layouts  14.8 us (6%)
    all_to_all x1, waiting for transfers between devices, per_device(): lax.all_to_all(outgoing, 'replica', split_axis=0, concat_axis=0, tiled=True)  43.8 us
    all_to_all x1, waiting for transfers between devices, per_device(): lax.all_to_all(sent_master, 'fsdp', split_axis=0, concat_axis=1, tiled=True)  39 us
    all_to_all x1, blocking collectives, per_device(): lax.all_to_all(product, 'replica', split_axis=0, concat_axis=0, tiled=True)  30.9 us
    dot_general x4, matrix products, orthogonalize(): jnp.dot(poly, state, preferred_element_type=jnp.float32)  21.9 us
    all_to_all x1, waiting for transfers between devices, per_device(): lax.all_to_all(sent_moment.astype(jnp.float32), 'fsdp', split_axis=0, con...  15.9 us
    dot_general x4, matrix products, orthogonalize(): lax.dot_general(state, state, (((1,), (1,)), ((), ())), preferred_element...  11.8 us
    all_to_all x1, starting transfers between devices, per_device(): lax.all_to_all(outgoing, 'replica', split_axis=0, concat_axis=0, tiled=True)  6.17 us
    dot_general x1, matrix products, per_device(): jnp.einsum('grd,od->gro', lax.all_to_all(outgoing, 'replica', split_axis=...  5.48 us
  transfers between devices with their start and end apart: 3, of which 3 were waited for; matrix products, arithmetic and copies ran while one was open for 28% of the time, Pallas kernels for 0%

commit v1 on v0

v1 whole, which is shorter than its diff:
```python
import functools
import math

import jax
import jax.numpy as jnp
from jax import lax
from jax.experimental import pallas as pl
from jax.experimental.pallas import tpu as pltpu
from jax.sharding import PartitionSpec as P

ITERS = 4


quintic_one = 3.4445
quintic_two = -4.775
quintic_three = 2.0315
learn_rate = 0.05
weight_decay = 0.1
norm_eps = 1e-07

ROW_BY_ROW = (((1,), (1,)), ((), ()))
ANY = pl.BlockSpec(memory_space=pl.ANY)
SMEM = pl.BlockSpec(memory_space=pltpu.SMEM)
VMEM = pl.BlockSpec(memory_space=pltpu.VMEM)


def partner(index, step, size):
    if size & (size - 1) == 0:
        return index ^ step
    return (index + step) % size


def source(index, step, size):
    if size & (size - 1) == 0:
        return index ^ step
    return (index + size - step) % size


def send(value, axis, step, size):
    return lax.ppermute(value, axis, [(i, partner(i, step, size)) for i in range(size)])


def send_back(value, axis, step, size):
    return lax.ppermute(value, axis, [(partner(i, step, size), i) for i in range(size)])


def far_first(size):
    half = size // 2
    evens = list(range(half, size, 2))
    odds = list(range(half + 1, size, 2))
    return evens + odds + list(range(half - 1, 0, -1))


def after(value, *others):
    return lax.optimization_barrier((value, *others))[0]


def pick_kernel(count, array_ref, index_ref, *rest):
    outs, sem = rest[-count - 1 : -1], rest[-1]
    copies = [
        pltpu.make_async_copy(array_ref.at[index_ref[k]], outs[k], sem.at[k])
        for k in range(count)
    ]
    for copy in copies:
        copy.start()
    for copy in copies:
        copy.wait()


def pick(array, index, count, *later_than):
    shape = array.shape[1:]
    size = math.prod(shape) * array.dtype.itemsize * count
    return pl.pallas_call(
        functools.partial(pick_kernel, count),
        out_shape=[jax.ShapeDtypeStruct(shape, array.dtype)] * count,
        in_specs=[ANY, SMEM] + [ANY] * len(later_than),
        out_specs=[VMEM] * count,
        scratch_shapes=[pltpu.SemaphoreType.DMA((count,))],
        cost_estimate=pl.CostEstimate(flops=0, bytes_accessed=2 * size, transcendentals=0),
        name="pick",
    )(array, index, *later_than)


def newton_kernel(chunk, place_ref, *rest):
    pieces, out_ref, poly_ref = rest[:-2], rest[-2], rest[-1]
    shard, width = pieces[0].shape
    total = jnp.float32(0.0)
    for piece in pieces:
        wide = piece[...].astype(jnp.float32)
        total += jnp.sum(wide * wide)
    scale = 1.0 / (jnp.sqrt(total) + norm_eps)
    for k, piece in enumerate(pieces):
        at = pl.ds(pl.multiple_of(place_ref[k] * shard, shard), shard)
        out_ref[at, :] = (piece[...].astype(jnp.float32) * scale).astype(jnp.bfloat16)

    def iteration(_, carry):
        state = out_ref[...]
        square = lax.dot_general(
            state, state, ROW_BY_ROW, preferred_element_type=jnp.float32
        ).astype(jnp.bfloat16)
        twice = jnp.dot(square, square, preferred_element_type=jnp.float32)
        poly_ref[...] = (
            quintic_two * square.astype(jnp.float32) + quintic_three * twice
        ).astype(jnp.bfloat16)

        def columns(c, carry):
            at = pl.ds(pl.multiple_of(c * chunk, chunk), chunk)
            part = out_ref[:, at]
            out_ref[:, at] = (
                quintic_one * part.astype(jnp.float32)
                + jnp.dot(poly_ref[...], part, preferred_element_type=jnp.float32)
            ).astype(jnp.bfloat16)
            return carry

        return lax.fori_loop(0, width // chunk, columns, carry)

    lax.fori_loop(0, ITERS, iteration, 0)


def orthogonalize(pieces, place):
    shard, width = pieces[0].shape
    rows = shard * len(pieces)
    chunk = 1024 if width % 1024 == 0 else width
    return pl.pallas_call(
        functools.partial(newton_kernel, chunk),
        out_shape=jax.ShapeDtypeStruct((rows, width), jnp.bfloat16),
        in_specs=[SMEM] + [VMEM] * len(pieces),
        out_specs=VMEM,
        scratch_shapes=[
            pltpu.VMEM((rows, rows), jnp.bfloat16),
        ],
        compiler_params=pltpu.CompilerParams(vmem_limit_bytes=40 << 20),
        cost_estimate=pl.CostEstimate(
            flops=ITERS * 2 * rows * rows * (2 * width + rows),
            bytes_accessed=4 * rows * width,
            transcendentals=0,
        ),
        name="newton",
    )(place, *pieces)


def per_device(weights, momentum, tokens, block_expert, owner_expert):
    owners = lax.axis_size("fsdp")
    groups = lax.axis_size("replica")
    group = lax.axis_index("replica")
    column = lax.axis_index("fsdp")
    blocks = block_expert.shape[0]
    width = tokens.shape[1]
    shard = weights.shape[1]
    rows = shard * owners
    resident = tokens.reshape(blocks, -1, width)
    target = block_expert // owners
    far = far_first(groups)
    steps = jnp.array(far + [0], jnp.int32)
    served = partner(group, steps, groups)
    slot = jnp.sum(
        jnp.where(
            target[None, :] == served[:, None], jnp.arange(blocks, dtype=jnp.int32)[None, :], 0
        ),
        axis=1,
    )
    table = lax.dynamic_slice_in_dim(owner_expert, group * owners, owners, 0) - group * owners
    near = list(range(owners - 1, -1, -1))
    near_steps = jnp.array(near, jnp.int32)
    local = table[partner(column, near_steps, owners)]
    place = source(column, near_steps, owners)

    arrived = {}
    first = pick(resident, slot[:2], 2)
    for k in range(2):
        arrived[k] = send(first[k], "replica", far[k], groups)
    parts = pick(momentum, local, owners)
    moment = [send(parts[k], "fsdp", near[k], owners) for k in range(owners - 1)] + [parts[-1]]

    second = pick(resident, slot[2:4], 2, *moment[:2])
    for k in range(2):
        arrived[2 + k] = send(second[k], "replica", far[2 + k], groups)
    kept = 1.0 - learn_rate * weight_decay
    decayed = [
        (lax.dynamic_index_in_dim(weights, local[k], 0, keepdims=False) * kept).astype(jnp.bfloat16)
        for k in range(owners)
    ]
    master = [send(after(decayed[k], *moment[:2]), "fsdp", near[k], owners) for k in range(owners - 1)]
    master.append(decayed[-1])
    update = orthogonalize(moment, place)
    third = pick(resident, slot[4:], groups - 4, master[0])
    for k in range(4, groups - 1):
        arrived[k] = send(third[k - 4], "replica", far[k], groups)
    arrived[groups - 1] = third[-1]

    whole = jnp.zeros((rows, width), jnp.bfloat16)
    for k in range(owners):
        whole = lax.dynamic_update_slice_in_dim(whole, master[k], place[k] * shard, 0)
    factor = learn_rate * 0.2 * math.sqrt(max(rows, width))
    refreshed = (
        whole.astype(jnp.float32) - factor * update.astype(jnp.float32)
    ).astype(jnp.bfloat16)
    fresh = refreshed[None]

    def product(block):
        return lax.dot_general(
            block, refreshed, ROW_BY_ROW, preferred_element_type=jnp.float32
        ).astype(jnp.bfloat16)

    answers = [
        send_back(product(arrived[k]), "replica", far[k], groups) for k in range(groups - 1)
    ]
    answers.append(product(arrived[groups - 1]))
    order = jnp.argmax(target[:, None] == served[None, :], axis=1)
    rollout = jnp.take(jnp.stack(answers), order, axis=0, mode="clip").reshape(-1, rows)
    return (fresh, rollout)


def solution(mesh):
    placed = (
        P("replica", "fsdp", None),
        P("replica", "fsdp", None),
        P(("fsdp", "replica"), None),
        P(("fsdp", "replica")),
        P(),
    )
    return jax.shard_map(
        per_device,
        mesh=mesh,
        in_specs=placed,
        out_specs=(P(("fsdp", "replica"), None, None), P(("fsdp", "replica"), None)),
        check_vma=False,
    )
```

time: 229 us -> 153 us (0.67); the launches traced: 225 us -> 153 us
  waiting for transfers between devices: 98.7 us -> 58.8 us
  matrix products: 44.9 us -> 8.74 us
  blocking collectives: 30.9 us -> 0 us
  Pallas kernels: 0 us -> 27 us
  starting transfers between devices: 15.6 us -> 28.5 us
  other arithmetic: 19.1 us -> 7.79 us
  between operations: 1.45 us -> 11.1 us
  local copies, waits for them, and re-layouts: 14.8 us -> 10.6 us
    all_to_all x3 -> x0, waiting for transfers between devices: 98.7 us -> none  [the longest x1 43.8 us: per_device(): lax.all_to_all(outgoing, 'replica', split_axis=0, concat_axis=0, tiled=True)]
    ppermute x0 -> x20, waiting for transfers between devices: none -> 58.8 us  [the longest x13 49.3 us: send(): lax.ppermute(value, axis, [(i, partner(i, step, size)) for i in range(siz...]
    dot_general x11 -> x8, matrix products: 44.9 us -> 8.74 us  [product(): lax.dot_general(block, refreshed, ROW_BY_ROW, preferred_element_type=jnp....]
    all_to_all x1 -> x0, blocking collectives: 30.9 us -> none  [per_device(): lax.all_to_all(product, 'replica', split_axis=0, concat_axis=0, tiled=True)]
    ppermute x0 -> x20, starting transfers between devices: none -> 28.5 us  [the longest x13 19 us: send(): lax.ppermute(value, axis, [(i, partner(i, step, size)) for i in range(siz...]
    pallas_call x0 -> x5, Pallas kernels: none -> 27 us  [the longest x1 14.2 us: orthogonalize(): pl.pallas_call(functools.partial(newton_kernel, chunk), out_shape=jax.Sha...]
    all_to_all x3 -> x0, starting transfers between devices: 15.6 us -> none  [the longest x1 6.17 us: per_device(): lax.all_to_all(outgoing, 'replica', split_axis=0, concat_axis=0, tiled=True)]
    convert_element_type x3 -> x0, local copies, waits for them, and re-layouts: 5.78 us -> none  [the longest x1 4.24 us: per_device(): outgoing = jnp.einsum('bg,brd->grd', selector, resident, preferred_elemen...]
  transfers between devices with their start and end apart: 3 -> 20, of which waited for: 3 -> 9; matrix products, arithmetic and copies ran while one was open for 28% -> 13% of each run, Pallas kernels for 0% -> 15%
where the time goes in v1:
time: 153 us
  waiting for transfers between devices  58.8 us (38%)
  starting transfers between devices  28.5 us (19%)
  Pallas kernels  27 us (18%)
  between operations  11.1 us (7%)
  local copies, waits for them, and re-layouts  10.6 us (7%)
  matrix products  8.74 us (6%)
  other arithmetic  7.79 us (5%)
    ppermute x13, waiting for transfers between devices, send(): lax.ppermute(value, axis, [(i, partner(i, step, size)) for i in range(siz...  49.3 us
    ppermute x13, starting transfers between devices, send(): lax.ppermute(value, axis, [(i, partner(i, step, size)) for i in range(siz...  19 us
    pallas_call x1, Pallas kernels, orthogonalize(): pl.pallas_call(functools.partial(newton_kernel, chunk), out_shape=jax.Sha...  14.2 us
    pallas_call x4, Pallas kernels, pick(): pl.pallas_call(functools.partial(pick_kernel, count), out_shape=[jax.Shap...  12.8 us
    ppermute x7, starting transfers between devices, send_back(): lax.ppermute(value, axis, [(partner(i, step, size), i) for i in range(siz...  9.55 us
    ppermute x7, waiting for transfers between devices, send_back(): lax.ppermute(value, axis, [(partner(i, step, size), i) for i in range(siz...  9.5 us
    dot_general x8, matrix products, product(): lax.dot_general(block, refreshed, ROW_BY_ROW, preferred_element_type=jnp....  8.74 us
    dynamic_update_slice x3, local copies, waits for them, and re-layouts, per_device(): lax.dynamic_update_slice_in_dim(whole, master[k], place[k] * shard, 0)  3.27 us
  transfers between devices with their start and end apart: 20, of which 9 were waited for; matrix products, arithmetic and copies ran while one was open for 13% of the time, Pallas kernels for 15%

profile of v1, /device:TPU:16, one launch (start us, length us, event | category | flops | bytes accessed | tf_op | source)
XLA Modules:
  0.0 152.5 jit_solution(9040660199445003970)
XLA Ops:
  3.2 3.5 %pick.4 = (bf16[128,2048]{1,0:T(8,128)(2,1)}, bf16[128,2048]{1,0:T(8,128)(2,1)}, bf16[128,2048]{1,0:T(8,128)(2,1)}, bf16[128,2048]{1,0:T(8,128)(2,1)}) custom-call(bf16[4,128,2048]{2,1,0:T(8,128)(2,1)} %array_ref.1, s32[4]{0:T(128)} %gather_fusion), custom_call_target="tpu_custom_call" | custom-call | bytes 4194304 | tf_op jit(solution)/shard_map/pick/pallas_call | solution.py:73
  9.5 2.9 %pick.5 = (bf16[128,2048]{1,0:T(8,128)(2,1)}, bf16[128,2048]{1,0:T(8,128)(2,1)}) custom-call(bf16[7,128,2048]{2,1,0:T(8,128)(2,1)} %bitcast.56, s32[2]{0:T(128)} %get-tuple-element.38.index_ref), custom_call_target="tpu_custom_call" | custom-call | bytes 2097152 | tf_op jit(solution)/shard_map/pick/pallas_call | solution.py:73
  12.5 3.0 %collective-permute-start.8 = (bf16[128,2048]{1,0:T(8,128)(2,1)}, bf16[128,2048]{1,0:T(8,128)(2,1)}, u32[]{:S(2)}, u32[]{:S(2)}) collective-permute-start(bf16[128,2048]{1,0:T(8,128)(2,1)} %get-tuple-element.26), channel_id=1, source_target_pairs={{0,6},{1,7},{2,4},{3,5},{4,2},{5,3},{6,0},{7,1},{8,14},{9,15},{10,... | collective-permute-start | bytes 1572872 | tf_op jit(solution)/shard_map/ppermute | solution.py:40
  28.1 3.2 %fusion.4 = (bf16[128,2048]{1,0:T(8,128)(2,1)}, bf16[128,2048]{1,0:T(8,128)(2,1)}, bf16[128,2048]{1,0:T(8,128)(2,1)}) fusion(f32[4,128,2048]{2,1,0:T(8,128)} %param.7, s32[]{:T(128)S(6)} %select_n.50, s32[]{:T(128)S(6)} %select_n.48, s32[]{:T(128)S(6)} %select_n.46), kind=kLoop, calls=%fused_computation.19 | loop fusion | flops 1572864 | bytes 4718604 | tf_op jit(solution)/shard_map/convert_element_type | solution.py:180
  36.2 14.2 %newton.1 = bf16[512,2048]{1,0:T(8,128)(2,1)S(1)} custom-call(s32[4]{0:T(128)S(1)} %get-tuple-element.48.place_ref, bf16[128,2048]{1,0:T(8,128)(2,1)S(1)} %collective-permute-done.rest_0_, bf16[128,2048]{1,0:T(8,128)(2,1)S(1)} %collective-permute-done.1.rest_1_, bf16[128,2048]{1,0:T(8,128)(2,1)S(1)} %copy-done.4, bf16[128,2048]{1,0:T(8,128)(2,1)S(1)} %copy-done.2), custom_call_target="tpu_custom_call" | custom-call | flops 9663676416 | bytes 4194304 | tf_op jit(solution)/shard_map/newton/pallas_call | solution.py:124
  50.4 2.9 %pick.6 = (bf16[128,2048]{1,0:T(8,128)(2,1)}, bf16[128,2048]{1,0:T(8,128)(2,1)}) custom-call(bf16[7,128,2048]{2,1,0:T(8,128)(2,1)} %bitcast.57, s32[2]{0:T(128)} %get-tuple-element.37.index_ref, bf16[128,2048]{1,0:T(8,128)(2,1)} %copy-done, bf16[128,2048]{1,0:T(8,128)(2,1)} %copy-done.1), custom_call_target="tpu_custom_call" | custom-call | bytes 2097152 | tf_op jit(solution)/shard_map/pick/pallas_call | solution.py:73
  53.3 1.4 collective-permute-start.10
  54.6 3.5 %pick.7 = (bf16[128,2048]{1,0:T(8,128)(2,1)}, bf16[128,2048]{1,0:T(8,128)(2,1)}, bf16[128,2048]{1,0:T(8,128)(2,1)}, bf16[128,2048]{1,0:T(8,128)(2,1)}) custom-call(bf16[7,128,2048]{2,1,0:T(8,128)(2,1)} %bitcast.58, s32[4]{0:T(128)} %slice.43.index_ref, bf16[128,2048]{1,0:T(8,128)(2,1)} %collective-permute-done.2.rest_0_), custom_call_target="tpu_custom_call" | custom-call | bytes 4194304 | tf_op jit(solution)/shard_map/pick/pallas_call | solution.py:73
  59.6 2.7 %collective-permute-start.12 = (bf16[128,2048]{1,0:T(8,128)(2,1)S(1)}, bf16[128,2048]{1,0:T(8,128)(2,1)S(1)}, u32[]{:S(2)}, u32[]{:S(2)}) collective-permute-start(bf16[128,2048]{1,0:T(8,128)(2,1)S(1)} %copy-done.11), channel_id=1, source_target_pairs={{0,7},{1,6},{2,5},{3,4},{4,3},{5,2},{6,1},{7,0},{8,15},{9,14},{10,... | collective-permute-start | bytes 1572872 | tf_op jit(solution)/shard_map/ppermute | solution.py:40
  63.4 2.4 %collective-permute-start.14 = (bf16[128,2048]{1,0:T(8,128)(2,1)S(1)}, bf16[128,2048]{1,0:T(8,128)(2,1)S(1)}, u32[]{:S(2)}, u32[]{:S(2)}) collective-permute-start(bf16[128,2048]{1,0:T(8,128)(2,1)S(1)} %copy-done.10), channel_id=1, source_target_pairs={{0,3},{1,2},{2,1},{3,0},{4,7},{5,6},{6,5},{7,4},{8,11},{9,10},{10,... | collective-permute-start | bytes 1572872 | tf_op jit(solution)/shard_map/ppermute | solution.py:40
  69.2 23.4 %collective-permute-done.10 = bf16[128,2048]{1,0:T(8,128)(2,1)S(1)} collective-permute-done((bf16[128,2048]{1,0:T(8,128)(2,1)}, bf16[128,2048]{1,0:T(8,128)(2,1)S(1)}, u32[]{:S(2)}, u32[]{:S(2)}) %collective-permute-start.10) | collective-permute-done | bytes 524320 | tf_op jit(solution)/shard_map/ppermute | solution.py:40
  93.4 4.2 %collective-permute-start.11 = (bf16[128,512]{1,0:T(8,128)(2,1)S(1)}, bf16[128,512]{1,0:T(8,128)(2,1)S(1)}, u32[]{:S(2)}, u32[]{:S(2)}) collective-permute-start(bf16[128,512]{1,0:T(8,128)(2,1)S(1)} %convolution_convert_fusion.5), channel_id=1, source_target_pairs={{5,0},{4,1},{7,2},{6,3},{1,4},{0,5},{3,6},{2,7},{13,8},{12,9},{15,... | collective-permute-start | bytes 393224 | tf_op jit(solution)/shard_map/ppermute | solution.py:44
  97.7 1.9 %convolution_convert_fusion.7 = bf16[128,512]{1,0:T(8,128)(2,1)S(1)} fusion(bf16[128,2048]{1,0:T(8,128)(2,1)} %collective-permute-done.6, bf16[512,2048]{1,0:T(8,128)(2,1)S(1)} %subtract_convert_fusion), kind=kOutput, calls=%fused_computation.10 | convolution fusion | flops 268500992 | bytes 2752512 | tf_op jit(solution)/shard_map/dot_general | solution.py:201
  100.0 1.9 %convolution_convert_fusion.6 = bf16[128,512]{1,0:T(8,128)(2,1)S(1)} fusion(bf16[128,2048]{1,0:T(8,128)(2,1)} %collective-permute-done.8, bf16[512,2048]{1,0:T(8,128)(2,1)S(1)} %subtract_convert_fusion), kind=kOutput, calls=%fused_computation.9 | convolution fusion | flops 268500992 | bytes 2752512 | tf_op jit(solution)/shard_map/dot_general | solution.py:201
  101.9 2.0 %collective-permute-start.9 = (bf16[128,512]{1,0:T(8,128)(2,1)S(1)}, bf16[128,512]{1,0:T(8,128)(2,1)S(1)}, u32[]{:S(2)}, u32[]{:S(2)}) collective-permute-start(bf16[128,512]{1,0:T(8,128)(2,1)S(1)} %convolution_convert_fusion.6), channel_id=1, source_target_pairs={{6,0},{7,1},{4,2},{5,3},{2,4},{3,5},{0,6},{1,7},{14,8},{15,9},{12,... | collective-permute-start | bytes 393224 | tf_op jit(solution)/shard_map/ppermute | solution.py:44
  103.9 14.7 %collective-permute-done.12 = bf16[128,2048]{1,0:T(8,128)(2,1)S(1)} collective-permute-done((bf16[128,2048]{1,0:T(8,128)(2,1)S(1)}, bf16[128,2048]{1,0:T(8,128)(2,1)S(1)}, u32[]{:S(2)}, u32[]{:S(2)}) %collective-permute-start.12) | collective-permute-done | bytes 524320 | tf_op jit(solution)/shard_map/ppermute | solution.py:40
  120.6 4.1 %collective-permute-start.16 = (bf16[128,2048]{1,0:T(8,128)(2,1)S(1)}, bf16[128,2048]{1,0:T(8,128)(2,1)S(1)}, u32[]{:S(2)}, u32[]{:S(2)}) collective-permute-start(bf16[128,2048]{1,0:T(8,128)(2,1)S(1)} %copy-done.9), channel_id=1, source_target_pairs={{0,2},{1,3},{2,0},{3,1},{4,6},{5,7},{6,4},{7,5},{8,10},{9,11},{10,... | collective-permute-start | bytes 1572872 | tf_op jit(solution)/shard_map/ppermute | solution.py:40
  126.0 1.5 collective-permute-start.18
  127.6 2.2 %collective-permute-done.13 = bf16[128,512]{1,0:T(8,128)(2,1)S(1)} collective-permute-done((bf16[128,512]{1,0:T(8,128)(2,1)S(1)}, bf16[128,512]{1,0:T(8,128)(2,1)S(1)}, u32[]{:S(2)}, u32[]{:S(2)}) %collective-permute-start.13) | collective-permute-done | bytes 131104 | tf_op jit(solution)/shard_map/ppermute | solution.py:44
  130.8 6.6 %collective-permute-done.16 = bf16[128,2048]{1,0:T(8,128)(2,1)S(1)} collective-permute-done((bf16[128,2048]{1,0:T(8,128)(2,1)S(1)}, bf16[128,2048]{1,0:T(8,128)(2,1)S(1)}, u32[]{:S(2)}, u32[]{:S(2)}) %collective-permute-start.16) | collective-permute-done | bytes 524320 | tf_op jit(solution)/shard_map/ppermute | solution.py:40
  138.3 2.1 %collective-permute-start.17 = (bf16[128,512]{1,0:T(8,128)(2,1)S(1)}, bf16[128,512]{1,0:T(8,128)(2,1)S(1)}, u32[]{:S(2)}, u32[]{:S(2)}) collective-permute-start(bf16[128,512]{1,0:T(8,128)(2,1)S(1)} %convolution_convert_fusion.2), channel_id=1, source_target_pairs={{2,0},{3,1},{0,2},{1,3},{6,4},{7,5},{4,6},{5,7},{10,8},{11,9},{8,1... | collective-permute-start | bytes 393224 | tf_op jit(solution)/shard_map/ppermute | solution.py:44
  140.4 3.4 %collective-permute-done.18 = bf16[128,2048]{1,0:T(8,128)(2,1)S(1)} collective-permute-done((bf16[128,2048]{1,0:T(8,128)(2,1)S(1)}, bf16[128,2048]{1,0:T(8,128)(2,1)S(1)}, u32[]{:S(2)}, u32[]{:S(2)}) %collective-permute-start.18) | collective-permute-done | bytes 524320 | tf_op jit(solution)/shard_map/ppermute | solution.py:40
  145.2 4.9 %collective-permute-done.19 = bf16[128,512]{1,0:T(8,128)(2,1)S(1)} collective-permute-done((bf16[128,512]{1,0:T(8,128)(2,1)S(1)}, bf16[128,512]{1,0:T(8,128)(2,1)S(1)}, u32[]{:S(2)}, u32[]{:S(2)}) %collective-permute-start.19) | collective-permute-done | bytes 131104 | tf_op jit(solution)/shard_map/ppermute | solution.py:44
  151.0 1.5 %gather_fusion.1 = bf16[7,128,512]{2,1,0:T(8,128)(2,1)} fusion(bf16[8,128,512]{2,1,0:T(8,128)(2,1)S(1)} %fusion.1, s32[1024]{0:T(1024)S(1)} %pad_clamp_fusion), kind=kCustom, calls=%fused_computation.1 | custom fusion | bytes 1835036 | tf_op jit(solution)/shard_map/jit(_take)/gather | solution.py:210
  (85 shorter events, 27.3 us)
Async XLA Ops:
  6.8 24.6 %collective-permute-start = (bf16[128,2048]{1,0:T(8,128)(2,1)}, bf16[128,2048]{1,0:T(8,128)(2,1)S(1)}, u32[]{:S(2)}, u32[]{:S(2)}) collective-permute-start(bf16[128,2048]{1,0:T(8,128)(2,1)} %get-tuple-element.18), channel_id=1, source_target_pairs={{0,24},{8,16},{16,8},{24,0},{1,25},{9,17},{17,9},{25,1},{2,26},{10... | collective-permute-start | bytes 1572872 | tf_op jit(solution)/shard_map/ppermute | solution.py:40
  7.8 24.7 %collective-permute-start.1 = (bf16[128,2048]{1,0:T(8,128)(2,1)}, bf16[128,2048]{1,0:T(8,128)(2,1)S(1)}, u32[]{:S(2)}, u32[]{:S(2)}) collective-permute-start(bf16[128,2048]{1,0:T(8,128)(2,1)} %get-tuple-element.19), channel_id=1, source_target_pairs={{0,16},{8,24},{16,0},{24,8},{1,17},{9,25},{17,1},{25,9},{2,18},{10... | collective-permute-start | bytes 1572872 | tf_op jit(solution)/shard_map/ppermute | solution.py:40
  8.4 25.8 %collective-permute-start.5 = (bf16[128,2048]{1,0:T(8,128)(2,1)}, bf16[128,2048]{1,0:T(8,128)(2,1)S(1)}, u32[]{:S(2)}, u32[]{:S(2)}) collective-permute-start(bf16[128,2048]{1,0:T(8,128)(2,1)} %get-tuple-element.23), channel_id=1, source_target_pairs={{0,8},{8,0},{16,24},{24,16},{1,9},{9,1},{17,25},{25,17},{2,10},{10... | collective-permute-start | bytes 1572872 | tf_op jit(solution)/shard_map/ppermute | solution.py:40
  12.4 85.3 %collective-permute-start.6 = (bf16[128,2048]{1,0:T(8,128)(2,1)}, bf16[128,2048]{1,0:T(8,128)(2,1)}, u32[]{:S(2)}, u32[]{:S(2)}) collective-permute-start(bf16[128,2048]{1,0:T(8,128)(2,1)} %get-tuple-element.25), channel_id=1, source_target_pairs={{0,4},{1,5},{2,6},{3,7},{4,0},{5,1},{6,2},{7,3},{8,12},{9,13},{10,... | collective-permute-start | bytes 1572872 | tf_op jit(solution)/shard_map/ppermute | solution.py:40
  12.5 87.4 %collective-permute-start.8 = (bf16[128,2048]{1,0:T(8,128)(2,1)}, bf16[128,2048]{1,0:T(8,128)(2,1)}, u32[]{:S(2)}, u32[]{:S(2)}) collective-permute-start(bf16[128,2048]{1,0:T(8,128)(2,1)} %get-tuple-element.26), channel_id=1, source_target_pairs={{0,6},{1,7},{2,4},{3,5},{4,2},{5,3},{6,0},{7,1},{8,14},{9,15},{10,... | collective-permute-start | bytes 1572872 | tf_op jit(solution)/shard_map/ppermute | solution.py:40
  31.3 19.0 %copy-start = (bf16[128,2048]{1,0:T(8,128)(2,1)}, bf16[128,2048]{1,0:T(8,128)(2,1)S(1)}, u32[]{:S(2)}) copy-start(bf16[128,2048]{1,0:T(8,128)(2,1)S(1)} %collective-permute-done.rest_0_) | copy-start | bytes 1572868
  32.5 20.8 %collective-permute-start.2 = (bf16[128,2048]{1,0:T(8,128)(2,1)}, bf16[128,2048]{1,0:T(8,128)(2,1)}, u32[]{:S(2)}, u32[]{:S(2)}) collective-permute-start(bf16[128,2048]{1,0:T(8,128)(2,1)} %get-tuple-element.20), channel_id=1, source_target_pairs={{0,24},{8,16},{16,8},{24,0},{1,25},{9,17},{17,9},{25,1},{2,26},{10... | collective-permute-start | bytes 1572872 | tf_op jit(solution)/shard_map/ppermute | solution.py:40
  33.7 25.9 %collective-permute-start.3 = (bf16[128,2048]{1,0:T(8,128)(2,1)}, bf16[128,2048]{1,0:T(8,128)(2,1)}, u32[]{:S(2)}, u32[]{:S(2)}) collective-permute-start(bf16[128,2048]{1,0:T(8,128)(2,1)} %get-tuple-element.21), channel_id=1, source_target_pairs={{0,16},{8,24},{16,0},{24,8},{1,17},{9,25},{17,1},{25,9},{2,18},{10... | collective-permute-start | bytes 1572872 | tf_op jit(solution)/shard_map/ppermute | solution.py:40
  35.0 28.4 %collective-permute-start.4 = (bf16[128,2048]{1,0:T(8,128)(2,1)}, bf16[128,2048]{1,0:T(8,128)(2,1)}, u32[]{:S(2)}, u32[]{:S(2)}) collective-permute-start(bf16[128,2048]{1,0:T(8,128)(2,1)} %get-tuple-element.22), channel_id=1, source_target_pairs={{0,8},{8,0},{16,24},{24,16},{1,9},{9,1},{17,25},{25,17},{2,10},{10... | collective-permute-start | bytes 1572872 | tf_op jit(solution)/shard_map/ppermute | solution.py:40
  53.3 39.3 %collective-permute-start.10 = (bf16[128,2048]{1,0:T(8,128)(2,1)}, bf16[128,2048]{1,0:T(8,128)(2,1)S(1)}, u32[]{:S(2)}, u32[]{:S(2)}) collective-permute-start(bf16[128,2048]{1,0:T(8,128)(2,1)} %get-tuple-element.27), channel_id=1, source_target_pairs={{0,5},{1,4},{2,7},{3,6},{4,1},{5,0},{6,3},{7,2},{8,13},{9,12},{10,... | collective-permute-start | bytes 1572872 | tf_op jit(solution)/shard_map/ppermute | solution.py:40
  59.6 59.0 %collective-permute-start.12 = (bf16[128,2048]{1,0:T(8,128)(2,1)S(1)}, bf16[128,2048]{1,0:T(8,128)(2,1)S(1)}, u32[]{:S(2)}, u32[]{:S(2)}) collective-permute-start(bf16[128,2048]{1,0:T(8,128)(2,1)S(1)} %copy-done.11), channel_id=1, source_target_pairs={{0,7},{1,6},{2,5},{3,4},{4,3},{5,2},{6,1},{7,0},{8,15},{9,14},{10,... | collective-permute-start | bytes 1572872 | tf_op jit(solution)/shard_map/ppermute | solution.py:40
  63.4 66.4 %collective-permute-start.14 = (bf16[128,2048]{1,0:T(8,128)(2,1)S(1)}, bf16[128,2048]{1,0:T(8,128)(2,1)S(1)}, u32[]{:S(2)}, u32[]{:S(2)}) collective-permute-start(bf16[128,2048]{1,0:T(8,128)(2,1)S(1)} %copy-done.10), channel_id=1, source_target_pairs={{0,3},{1,2},{2,1},{3,0},{4,7},{5,6},{6,5},{7,4},{8,11},{9,10},{10,... | collective-permute-start | bytes 1572872 | tf_op jit(solution)/shard_map/ppermute | solution.py:40
  69.2 81.0 %copy-start.5 = (bf16[512,2048]{1,0:T(8,128)(2,1)}, bf16[512,2048]{1,0:T(8,128)(2,1)S(1)}, u32[]{:S(2)}) copy-start(bf16[512,2048]{1,0:T(8,128)(2,1)S(1)} %subtract_convert_fusion) | copy-start | bytes 6291460
  93.4 34.2 %collective-permute-start.11 = (bf16[128,512]{1,0:T(8,128)(2,1)S(1)}, bf16[128,512]{1,0:T(8,128)(2,1)S(1)}, u32[]{:S(2)}, u32[]{:S(2)}) collective-permute-start(bf16[128,512]{1,0:T(8,128)(2,1)S(1)} %convolution_convert_fusion.5), channel_id=1, source_target_pairs={{5,0},{4,1},{7,2},{6,3},{1,4},{0,5},{3,6},{2,7},{13,8},{12,9},{15,... | collective-permute-start | bytes 393224 | tf_op jit(solution)/shard_map/ppermute | solution.py:44
  99.5 21.0 %copy-start.9 = (bf16[128,2048]{1,0:T(8,128)(2,1)S(1)}, bf16[128,2048]{1,0:T(8,128)(2,1)}, u32[]{:S(2)}) copy-start(bf16[128,2048]{1,0:T(8,128)(2,1)} %get-tuple-element.30) | copy-start | bytes 1572868
  99.5 21.0 %collective-permute-start.7 = (bf16[128,512]{1,0:T(8,128)(2,1)S(1)}, bf16[128,512]{1,0:T(8,128)(2,1)S(1)}, u32[]{:S(2)}, u32[]{:S(2)}) collective-permute-start(bf16[128,512]{1,0:T(8,128)(2,1)S(1)} %convolution_convert_fusion.7), channel_id=1, source_target_pairs={{4,0},{5,1},{6,2},{7,3},{0,4},{1,5},{2,6},{3,7},{12,8},{13,9},{14,... | collective-permute-start | bytes 393224 | tf_op jit(solution)/shard_map/ppermute | solution.py:44
  101.8 24.2 %copy-start.8 = (bf16[128,2048]{1,0:T(8,128)(2,1)S(1)}, bf16[128,2048]{1,0:T(8,128)(2,1)}, u32[]{:S(2)}) copy-start(bf16[128,2048]{1,0:T(8,128)(2,1)} %get-tuple-element.31) | copy-start | bytes 1572868
  101.9 24.2 %collective-permute-start.9 = (bf16[128,512]{1,0:T(8,128)(2,1)S(1)}, bf16[128,512]{1,0:T(8,128)(2,1)S(1)}, u32[]{:S(2)}, u32[]{:S(2)}) collective-permute-start(bf16[128,512]{1,0:T(8,128)(2,1)S(1)} %convolution_convert_fusion.6), channel_id=1, source_target_pairs={{6,0},{7,1},{4,2},{5,3},{2,4},{3,5},{0,6},{1,7},{14,8},{15,9},{12,... | collective-permute-start | bytes 393224 | tf_op jit(solution)/shard_map/ppermute | solution.py:44
  119.4 10.4 %collective-permute-start.13 = (bf16[128,512]{1,0:T(8,128)(2,1)S(1)}, bf16[128,512]{1,0:T(8,128)(2,1)S(1)}, u32[]{:S(2)}, u32[]{:S(2)}) collective-permute-start(bf16[128,512]{1,0:T(8,128)(2,1)S(1)} %convolution_convert_fusion.4), channel_id=1, source_target_pairs={{7,0},{6,1},{5,2},{4,3},{3,4},{2,5},{1,6},{0,7},{15,8},{14,9},{13,... | collective-permute-start | bytes 393224 | tf_op jit(solution)/shard_map/ppermute | solution.py:44
  120.6 16.9 %collective-permute-start.16 = (bf16[128,2048]{1,0:T(8,128)(2,1)S(1)}, bf16[128,2048]{1,0:T(8,128)(2,1)S(1)}, u32[]{:S(2)}, u32[]{:S(2)}) collective-permute-start(bf16[128,2048]{1,0:T(8,128)(2,1)S(1)} %copy-done.9), channel_id=1, source_target_pairs={{0,2},{1,3},{2,0},{3,1},{4,6},{5,7},{6,4},{7,5},{8,10},{9,11},{10,... | collective-permute-start | bytes 1572872 | tf_op jit(solution)/shard_map/ppermute | solution.py:40
  126.0 17.7 %collective-permute-start.18 = (bf16[128,2048]{1,0:T(8,128)(2,1)S(1)}, bf16[128,2048]{1,0:T(8,128)(2,1)S(1)}, u32[]{:S(2)}, u32[]{:S(2)}) collective-permute-start(bf16[128,2048]{1,0:T(8,128)(2,1)S(1)} %copy-done.8), channel_id=1, source_target_pairs={{0,1},{1,0},{2,3},{3,2},{4,5},{5,4},{6,7},{7,6},{8,9},{9,8},{10,11... | collective-permute-start | bytes 1572872 | tf_op jit(solution)/shard_map/ppermute | solution.py:40
  130.7 14.5 %collective-permute-start.15 = (bf16[128,512]{1,0:T(8,128)(2,1)S(1)}, bf16[128,512]{1,0:T(8,128)(2,1)S(1)}, u32[]{:S(2)}, u32[]{:S(2)}) collective-permute-start(bf16[128,512]{1,0:T(8,128)(2,1)S(1)} %convolution_convert_fusion.3), channel_id=1, source_target_pairs={{3,0},{2,1},{1,2},{0,3},{7,4},{6,5},{5,6},{4,7},{11,8},{10,9},{9,1... | collective-permute-start | bytes 393224 | tf_op jit(solution)/shard_map/ppermute | solution.py:44
  138.3 6.9 %collective-permute-start.17 = (bf16[128,512]{1,0:T(8,128)(2,1)S(1)}, bf16[128,512]{1,0:T(8,128)(2,1)S(1)}, u32[]{:S(2)}, u32[]{:S(2)}) collective-permute-start(bf16[128,512]{1,0:T(8,128)(2,1)S(1)} %convolution_convert_fusion.2), channel_id=1, source_target_pairs={{2,0},{3,1},{0,2},{1,3},{6,4},{7,5},{4,6},{5,7},{10,8},{11,9},{8,1... | collective-permute-start | bytes 393224 | tf_op jit(solution)/shard_map/ppermute | solution.py:44
  144.6 5.5 %collective-permute-start.19 = (bf16[128,512]{1,0:T(8,128)(2,1)S(1)}, bf16[128,512]{1,0:T(8,128)(2,1)S(1)}, u32[]{:S(2)}, u32[]{:S(2)}) collective-permute-start(bf16[128,512]{1,0:T(8,128)(2,1)S(1)} %convolution_convert_fusion.1), channel_id=1, source_target_pairs={{1,0},{0,1},{3,2},{2,3},{5,4},{4,5},{7,6},{6,7},{9,8},{8,9},{11,10... | collective-permute-start | bytes 393224 | tf_op jit(solution)/shard_map/ppermute | solution.py:44
  (10 other events, 70.1 us)

commit v2 on v1

v2 whole, which is shorter than its diff:
```python
import functools
import math

import jax
import jax.numpy as jnp
from jax import lax
from jax.experimental import pallas as pl
from jax.experimental.pallas import tpu as pltpu
from jax.sharding import PartitionSpec as P

ITERS = 4


quintic_one = 3.4445
quintic_two = -4.775
quintic_three = 2.0315
learn_rate = 0.05
weight_decay = 0.1
norm_eps = 1e-07

ROW_BY_ROW = (((1,), (1,)), ((), ()))
ANY = pl.BlockSpec(memory_space=pl.ANY)
SMEM = pl.BlockSpec(memory_space=pltpu.SMEM)
VMEM = pl.BlockSpec(memory_space=pltpu.VMEM)


def partner(index, step, size):
    if size & (size - 1) == 0:
        return index ^ step
    return (index + step) % size


def source(index, step, size):
    if size & (size - 1) == 0:
        return index ^ step
    return (index + size - step) % size


def send(value, axis, step, size):
    return lax.ppermute(value, axis, [(i, partner(i, step, size)) for i in range(size)])


def send_back(value, axis, step, size):
    return lax.ppermute(value, axis, [(partner(i, step, size), i) for i in range(size)])


def after(value, *others):
    return lax.optimization_barrier((value, *others))[0]


def pick_blocks_kernel(steps, groups, owners, tokens_ref, named_ref, *rest):
    outs, sem = rest[-1 - len(steps) : -1], rest[-1]
    group = lax.axis_index("replica")
    copies = []
    for k, step in enumerate(steps):
        wanted = partner(group, step, groups)
        slot = jnp.int32(0)
        for b in range(tokens_ref.shape[0]):
            slot = jnp.where(lax.div(named_ref[b], jnp.int32(owners)) == wanted, b, slot)
        copies.append(pltpu.make_async_copy(tokens_ref.at[slot], outs[k], sem.at[k]))
    for copy in copies:
        copy.start()
    for copy in copies:
        copy.wait()


def pick_blocks(resident, named, steps, groups, owners, *later_than):
    shape = resident.shape[1:]
    size = math.prod(shape) * resident.dtype.itemsize * len(steps)
    return pl.pallas_call(
        functools.partial(pick_blocks_kernel, steps, groups, owners),
        out_shape=[jax.ShapeDtypeStruct(shape, resident.dtype)] * len(steps),
        in_specs=[ANY, SMEM] + [ANY] * len(later_than),
        out_specs=[VMEM] * len(steps),
        scratch_shapes=[pltpu.SemaphoreType.DMA((len(steps),))],
        compiler_params=pltpu.CompilerParams(vmem_limit_bytes=56 << 20),
        cost_estimate=pl.CostEstimate(flops=0, bytes_accessed=2 * size, transcendentals=0),
        name="pick_blocks",
    )(resident, named, *later_than)


def block_of(group, named_ref, blocks, owners):
    slot = jnp.int32(0)
    for b in range(blocks):
        slot = jnp.where(lax.div(named_ref[b], jnp.int32(owners)) == group, b, slot)
    return slot


def lead_kernel(steps, groups, owners, tokens_ref, moment_ref, named_ref, owner_ref, *rest):
    outs, moment_out, sem = rest[: len(steps)], rest[-2], rest[-1]
    group = lax.axis_index("replica")
    first = group * owners
    copies = []
    for k, step in enumerate(steps):
        slot = block_of(partner(group, step, groups), named_ref, tokens_ref.shape[0], owners)
        copies.append(pltpu.make_async_copy(tokens_ref.at[slot], outs[k], sem.at[k]))
        copies[-1].start()
    for p in range(owners):
        copies.append(
            pltpu.make_async_copy(
                moment_ref.at[owner_ref[first + p] - first], moment_out.at[p], sem.at[len(steps) + p]
            )
        )
        copies[-1].start()
    for copy in copies:
        copy.wait()


def lead_pick(resident, momentum, named, owner_expert, steps, groups):
    owners = momentum.shape[0]
    shape = resident.shape[1:]
    out = pl.pallas_call(
        functools.partial(lead_kernel, steps, groups, owners),
        out_shape=[jax.ShapeDtypeStruct(shape, resident.dtype)] * len(steps)
        + [jax.ShapeDtypeStruct(momentum.shape, momentum.dtype)],
        in_specs=[ANY, ANY, SMEM, SMEM],
        out_specs=[VMEM] * (1 + len(steps)),
        scratch_shapes=[pltpu.SemaphoreType.DMA((len(steps) + owners,))],
        compiler_params=pltpu.CompilerParams(vmem_limit_bytes=56 << 20),
        cost_estimate=pl.CostEstimate(
            flops=0, bytes_accessed=4 * (momentum.size + len(steps) * math.prod(shape)), transcendentals=0
        ),
        name="lead_pick",
    )(resident, momentum, named, owner_expert)
    return out[:-1], out[-1]


def by_owner_kernel(owners, scale, later, array_ref, owner_ref, *rest):
    out_ref, *scratch = rest[later:]
    held, sem = (out_ref, scratch[0]) if scale is None else scratch
    first = lax.axis_index("replica") * owners
    copies = [
        pltpu.make_async_copy(array_ref.at[owner_ref[first + p] - first], held.at[p], sem.at[p])
        for p in range(owners)
    ]
    for copy in copies:
        copy.start()
    for p, copy in enumerate(copies):
        copy.wait()
        if scale is not None:
            out_ref[p] = (held[p] * scale).astype(out_ref.dtype)


def by_owner(array, owner_expert, scale, *later_than):
    owners = array.shape[0]
    scratch = [pltpu.SemaphoreType.DMA((owners,))]
    if scale is not None:
        scratch = [pltpu.VMEM(array.shape, array.dtype)] + scratch
    return pl.pallas_call(
        functools.partial(by_owner_kernel, owners, scale, len(later_than)),
        out_shape=jax.ShapeDtypeStruct(array.shape, jnp.bfloat16),
        in_specs=[ANY, SMEM] + [ANY] * len(later_than),
        out_specs=VMEM,
        scratch_shapes=scratch,
        compiler_params=pltpu.CompilerParams(vmem_limit_bytes=56 << 20),
        cost_estimate=pl.CostEstimate(
            flops=0, bytes_accessed=array.size * (array.dtype.itemsize + 2), transcendentals=0
        ),
        name="by_owner",
    )(array, owner_expert, *later_than)


def newton_kernel(chunk, moment_ref, *rest):
    out_ref, poly_ref = rest[-2:]
    width = moment_ref.shape[1]
    wide = moment_ref[...].astype(jnp.float32)
    scale = 1.0 / (jnp.sqrt(jnp.sum(wide * wide)) + norm_eps)
    out_ref[...] = (moment_ref[...].astype(jnp.float32) * scale).astype(jnp.bfloat16)

    def iteration(_, carry):
        state = out_ref[...]
        square = lax.dot_general(
            state, state, ROW_BY_ROW, preferred_element_type=jnp.float32
        ).astype(jnp.bfloat16)
        twice = jnp.dot(square, square, preferred_element_type=jnp.float32)
        poly_ref[...] = (
            quintic_two * square.astype(jnp.float32) + quintic_three * twice
        ).astype(jnp.bfloat16)

        def columns(c, carry):
            at = pl.ds(pl.multiple_of(c * chunk, chunk), chunk)
            part = out_ref[:, at]
            out_ref[:, at] = (
                quintic_one * part.astype(jnp.float32)
                + jnp.dot(poly_ref[...], part, preferred_element_type=jnp.float32)
            ).astype(jnp.bfloat16)
            return carry

        return lax.fori_loop(0, width // chunk, columns, carry)

    lax.fori_loop(0, ITERS, iteration, 0)


def orthogonalize(moment, *later_than):
    rows, width = moment.shape
    chunk = 1024 if width % 1024 == 0 else width
    return pl.pallas_call(
        functools.partial(newton_kernel, chunk),
        out_shape=jax.ShapeDtypeStruct((rows, width), jnp.bfloat16),
        in_specs=[VMEM] + [ANY] * len(later_than),
        out_specs=VMEM,
        scratch_shapes=[pltpu.VMEM((rows, rows), jnp.bfloat16)],
        compiler_params=pltpu.CompilerParams(vmem_limit_bytes=56 << 20),
        cost_estimate=pl.CostEstimate(
            flops=ITERS * 2 * rows * rows * (2 * width + rows),
            bytes_accessed=4 * rows * width,
            transcendentals=0,
        ),
        name="newton",
    )(moment, *later_than)


def refresh_kernel(factor, update_ref, master_ref, *rest):
    rest[-1][...] = (
        master_ref[...].astype(jnp.float32) - factor * update_ref[...].astype(jnp.float32)
    ).astype(jnp.bfloat16)


def refresh(update, master, *later_than):
    factor = learn_rate * 0.2 * math.sqrt(max(update.shape))
    return pl.pallas_call(
        functools.partial(refresh_kernel, factor),
        out_shape=jax.ShapeDtypeStruct(update.shape, jnp.bfloat16),
        in_specs=[VMEM] * 2 + [ANY] * len(later_than),
        out_specs=VMEM,
        compiler_params=pltpu.CompilerParams(vmem_limit_bytes=32 << 20),
        cost_estimate=pl.CostEstimate(
            flops=2 * update.size, bytes_accessed=6 * update.size, transcendentals=0
        ),
        name="refresh",
    )(update, master, *later_than)


def per_device(weights, momentum, tokens, block_expert, owner_expert):
    owners = lax.axis_size("fsdp")
    groups = lax.axis_size("replica")
    group = lax.axis_index("replica")
    blocks = block_expert.shape[0]
    width = tokens.shape[1]
    rows = weights.shape[1] * owners
    resident = tokens.reshape(blocks, -1, width)
    half = groups // 2
    far = list(range(half, groups, 2)) + list(range(half + 1, groups, 2))
    near = list(range(1, half))
    arrived = {}

    def pick(chosen, *later_than):
        return pick_blocks(resident, block_expert, chosen, groups, owners, *later_than)

    def send_all(blocks, chosen):
        for block, step in zip(blocks, chosen):
            arrived[step] = send(block, "replica", step, groups)

    lead, trail = far[: half // 2], far[half // 2 :]
    first, outgoing = lead_pick(resident, momentum, block_expert, owner_expert, lead, groups)
    send_all(first, lead)
    moment = lax.all_to_all(outgoing, "fsdp", 0, 0, tiled=True)
    second = pick(near, first[0])
    send_all(second, near)
    third = pick(trail + [0], arrived[near[0]])
    send_all(third, trail)
    arrived[0] = third[-1]
    kept = 1.0 - learn_rate * weight_decay
    master = lax.all_to_all(by_owner(weights, owner_expert, kept, moment), "fsdp", 0, 0, tiled=True)
    update = orthogonalize(moment.reshape(rows, width), third[0], *[arrived[step] for step in near])
    refreshed = refresh(update, master.reshape(rows, width), *[arrived[step] for step in lead])

    def product(block):
        return lax.dot_general(
            block, refreshed, ROW_BY_ROW, preferred_element_type=jnp.float32
        ).astype(jnp.bfloat16)

    answer = {0: product(arrived[0])}
    for step in near + lead + trail:
        answer[step] = send_back(product(arrived[step]), "replica", step, groups)
    steps = list(answer)
    served = partner(group, jnp.array(steps, jnp.int32), groups)
    order = jnp.argmax((block_expert // owners)[:, None] == served[None, :], axis=1)
    answers = jnp.stack([answer[step] for step in steps])
    rollout = jnp.take(answers, order, axis=0, mode="clip").reshape(-1, rows)
    return (refreshed[None], rollout)


def solution(mesh):
    placed = (
        P("replica", "fsdp", None),
        P("replica", "fsdp", None),
        P(("fsdp", "replica"), None),
        P(("fsdp", "replica")),
        P(),
    )
    return jax.shard_map(
        per_device,
        mesh=mesh,
        in_specs=placed,
        out_specs=(P(("fsdp", "replica"), None, None), P(("fsdp", "replica"), None)),
        check_vma=False,
    )
```

time: 153 us -> 129 us (0.84)
  between operations: 11.1 us -> 0.92 us
  waiting for transfers between devices: 58.8 us -> 48.7 us
  other arithmetic: 7.79 us -> 0.75 us
  Pallas kernels: 27 us -> 33.8 us
  local copies, waits for them, and re-layouts: 10.6 us -> 4.54 us
  matrix products: 8.74 us -> 12.9 us
  starting transfers between devices: 28.5 us -> 26.2 us
    ppermute x13 -> x7, waiting for transfers between devices: 49.3 us -> 20.4 us  [send(): lax.ppermute(value, axis, [(i, partner(i, step, size)) for i in range(siz...]
    all_to_all x0 -> x2, waiting for transfers between devices: none -> 15.8 us  [the longest x1 15.8 us: per_device(): moment = lax.all_to_all(outgoing, 'fsdp', 0, 0, tiled=True)]
    ppermute x13 -> x7, starting transfers between devices: 19 us -> 10.7 us  [send(): lax.ppermute(value, axis, [(i, partner(i, step, size)) for i in range(siz...]
    all_to_all x0 -> x2, starting transfers between devices: none -> 7.24 us  [the longest x1 3.62 us: per_device(): moment = lax.all_to_all(outgoing, 'fsdp', 0, 0, tiled=True)]
    convert_element_type x2 -> x0, other arithmetic: 4.16 us -> none  [the longest x1 3.2 us: per_device(): (lax.dynamic_index_in_dim(weights, local[k], 0, keepdims=False) * kept).a...]
    dot_general x8, matrix products: 8.74 us -> 12.9 us  [product(): lax.dot_general(block, refreshed, ROW_BY_ROW, preferred_element_type=jnp....]
    pallas_call x4 -> x5, Pallas kernels: 12.8 us -> 16.9 us  [the longest x2 6.43 us: pick_blocks(): pl.pallas_call(functools.partial(pick_blocks_kernel, steps, groups, owner...]
    dynamic_update_slice x3 -> x0, local copies, waits for them, and re-layouts: 3.27 us -> none  [per_device(): lax.dynamic_update_slice_in_dim(whole, master[k], place[k] * shard, 0)]
  transfers between devices with their start and end apart: 20 -> 16, of which waited for: 9 -> 6; matrix products, arithmetic and copies ran while one was open for 13% -> 11% of each run, Pallas kernels for 15% -> 23%
where the time goes in v2:
time: 129 us; the launch traced here: 128 us
  waiting for transfers between devices  48.7 us (38%)
  Pallas kernels  33.8 us (26%)
  starting transfers between devices  26.2 us (20%)
  matrix products  12.9 us (10%)
  local copies, waits for them, and re-layouts  4.54 us (4%)
    ppermute x7, waiting for transfers between devices, send(): lax.ppermute(value, axis, [(i, partner(i, step, size)) for i in range(siz...  20.4 us
    pallas_call x1, Pallas kernels, orthogonalize(): pl.pallas_call(functools.partial(newton_kernel, chunk), out_shape=jax.Sha...  16.9 us
    all_to_all x1, waiting for transfers between devices, per_device(): moment = lax.all_to_all(outgoing, 'fsdp', 0, 0, tiled=True)  15.8 us
    dot_general x8, matrix products, product(): lax.dot_general(block, refreshed, ROW_BY_ROW, preferred_element_type=jnp....  12.9 us
    ppermute x7, waiting for transfers between devices, send_back(): lax.ppermute(value, axis, [(partner(i, step, size), i) for i in range(siz...  12.6 us
    ppermute x7, starting transfers between devices, send(): lax.ppermute(value, axis, [(i, partner(i, step, size)) for i in range(siz...  10.7 us
    ppermute x7, starting transfers between devices, send_back(): lax.ppermute(value, axis, [(partner(i, step, size), i) for i in range(siz...  8.27 us
    pallas_call x2, Pallas kernels, pick_blocks(): pl.pallas_call(functools.partial(pick_blocks_kernel, steps, groups, owner...  6.43 us
  transfers between devices with their start and end apart: 16, of which 6 were waited for; matrix products, arithmetic and copies ran while one was open for 11% of the time, Pallas kernels for 23%

profile of v2, /device:TPU:16, one launch (start us, length us, event | category | flops | bytes accessed | tf_op | source)
XLA Modules:
  0.0 127.8 jit_solution(672698522896235642)
XLA Ops:
  0.6 4.2 %lead_pick.1 = (bf16[128,2048]{1,0:T(8,128)(2,1)}, bf16[128,2048]{1,0:T(8,128)(2,1)}, bf16[4,128,2048]{2,1,0:T(8,128)(2,1)}) custom-call(bf16[7,128,2048]{2,1,0:T(8,128)(2,1)} %bitcast.41, bf16[4,128,2048]{2,1,0:T(8,128)(2,1)} %moment_ref.1, s32[7]{0:T(128)} %named_ref.5, s32[32]{0:T(128)} %owner_ref.3), custom_call_target="tpu_custom_call" | custom-call | bytes 6291456 | tf_op jit(solution)/shard_map/lead_pick/pallas_call | solution.py:112
  4.9 3.6 %all-to-all-start = ((bf16[4,128,2048]{2,1,0:T(8,128)(2,1)}), bf16[4,128,2048]{2,1,0:T(8,128)(2,1)S(1)}, u32[]{:S(2)}, u32[]{:S(2)}) async-start(bf16[4,128,2048]{2,1,0:T(8,128)(2,1)} %get-tuple-element.12), calls=%async_computation | async-start | bytes 4194304 | tf_op jit(solution)/shard_map/all_to_all | solution.py:257
  8.6 3.2 %pick_blocks.2 = (bf16[128,2048]{1,0:T(8,128)(2,1)}, bf16[128,2048]{1,0:T(8,128)(2,1)}, bf16[128,2048]{1,0:T(8,128)(2,1)}) custom-call(bf16[7,128,2048]{2,1,0:T(8,128)(2,1)} %bitcast.42, s32[7]{0:T(128)} %named_ref.5, bf16[128,2048]{1,0:T(8,128)(2,1)} %get-tuple-element.13.rest_0_), custom_call_target="tpu_custom_call" | custom-call | bytes 3145728 | tf_op jit(solution)/shard_map/pick_blocks/pallas_call | solution.py:70
  11.8 1.9 %collective-permute-start = (bf16[128,2048]{1,0:T(8,128)(2,1)}, bf16[128,2048]{1,0:T(8,128)(2,1)}, u32[]{:S(2)}, u32[]{:S(2)}) collective-permute-start(bf16[128,2048]{1,0:T(8,128)(2,1)} %get-tuple-element.14), channel_id=1, source_target_pairs={{0,1},{1,0},{2,3},{3,2},{4,5},{5,4},{6,7},{7,6},{8,9},{9,8},{10,11... | collective-permute-start | bytes 1572872 | tf_op jit(solution)/shard_map/ppermute | solution.py:40
  15.4 3.0 %collective-permute-start.4 = (bf16[128,2048]{1,0:T(8,128)(2,1)}, bf16[128,2048]{1,0:T(8,128)(2,1)S(1)}, u32[]{:S(2)}, u32[]{:S(2)}) collective-permute-start(bf16[128,2048]{1,0:T(8,128)(2,1)} %get-tuple-element.18), channel_id=1, source_target_pairs={{0,6},{1,7},{2,4},{3,5},{4,2},{5,3},{6,0},{7,1},{8,14},{9,15},{10,... | collective-permute-start | bytes 1572872 | tf_op jit(solution)/shard_map/ppermute | solution.py:40
  18.4 15.8 %all-to-all-done.rest_0_ = bf16[4,128,2048]{2,1,0:T(8,128)(2,1)S(1)} async-done(((bf16[4,128,2048]{2,1,0:T(8,128)(2,1)}), bf16[4,128,2048]{2,1,0:T(8,128)(2,1)S(1)}, u32[]{:S(2)}, u32[]{:S(2)}) %all-to-all-start) | async-done | bytes 2097184 | tf_op jit(solution)/shard_map/all_to_all | solution.py:257
  35.5 4.3 %by_owner.1 = bf16[4,128,2048]{2,1,0:T(8,128)(2,1)} custom-call(f32[4,128,2048]{2,1,0:T(8,128)} %array_ref.1, s32[32]{0:T(128)} %owner_ref.3, bf16[4,128,2048]{2,1,0:T(8,128)(2,1)} %copy-done.2), custom_call_target="tpu_custom_call" | custom-call | bytes 6291456 | tf_op jit(solution)/shard_map/by_owner/pallas_call | solution.py:149
  39.8 3.6 %all-to-all-start.1 = ((bf16[4,128,2048]{2,1,0:T(8,128)(2,1)}), bf16[4,128,2048]{2,1,0:T(8,128)(2,1)S(1)}, u32[]{:S(2)}, u32[]{:S(2)}) async-start(bf16[4,128,2048]{2,1,0:T(8,128)(2,1)} %by_owner.1), calls=%async_computation.1 | async-start | bytes 4194304 | tf_op jit(solution)/shard_map/all_to_all | solution.py:264
  44.2 3.2 %pick_blocks.3 = (bf16[128,2048]{1,0:T(8,128)(2,1)}, bf16[128,2048]{1,0:T(8,128)(2,1)}, bf16[128,2048]{1,0:T(8,128)(2,1)}) custom-call(bf16[7,128,2048]{2,1,0:T(8,128)(2,1)} %bitcast.43, s32[7]{0:T(128)} %named_ref.5, bf16[128,2048]{1,0:T(8,128)(2,1)} %collective-permute-done.rest_0_.rest_1_), custom_call_target="tpu_custom_call" | custom-call | bytes 3145728 | tf_op jit(solution)/shard_map/pick_blocks/pallas_call | solution.py:70
  48.8 2.6 %collective-permute-start.12 = (bf16[128,2048]{1,0:T(8,128)(2,1)}, bf16[128,2048]{1,0:T(8,128)(2,1)}, u32[]{:S(2)}, u32[]{:S(2)}) collective-permute-start(bf16[128,2048]{1,0:T(8,128)(2,1)} %get-tuple-element.20), channel_id=1, source_target_pairs={{0,7},{1,6},{2,5},{3,4},{4,3},{5,2},{6,1},{7,0},{8,15},{9,14},{10,... | collective-permute-start | bytes 1572872 | tf_op jit(solution)/shard_map/ppermute | solution.py:40
  51.5 9.1 %collective-permute-done.2.rest_3_ = bf16[128,2048]{1,0:T(8,128)(2,1)} collective-permute-done((bf16[128,2048]{1,0:T(8,128)(2,1)}, bf16[128,2048]{1,0:T(8,128)(2,1)}, u32[]{:S(2)}, u32[]{:S(2)}) %collective-permute-start.2) | collective-permute-done | bytes 524320 | tf_op jit(solution)/shard_map/ppermute | solution.py:40
  60.5 16.9 %newton.1.update_ref = bf16[512,2048]{1,0:T(8,128)(2,1)} custom-call(bf16[512,2048]{1,0:T(8,128)(2,1)} %bitcast.44, bf16[128,2048]{1,0:T(8,128)(2,1)} %get-tuple-element.15.rest_0_, bf16[128,2048]{1,0:T(8,128)(2,1)} %collective-permute-done.rest_0_.rest_1_, bf16[128,2048]{1,0:T(8,128)(2,1)} %collective-permute-done.1.rest_2_, ...), custom_call_target="tpu_custom_call" | custom-call | flops 9663676416 | bytes 4194304 | tf_op jit(solution)/shard_map/newton/pallas_call | solution.py:197
  79.0 1.9 %refresh.1 = bf16[512,2048]{1,0:T(8,128)(2,1)} custom-call(bf16[512,2048]{1,0:T(8,128)(2,1)S(1)} %copy-done, bf16[512,2048]{1,0:T(8,128)(2,1)S(1)} %bitcast.39, bf16[128,2048]{1,0:T(8,128)(2,1)S(1)} %collective-permute-done.3.rest_0_, bf16[128,2048]{1,0:T(8,128)(2,1)S(1)} %collective-permute-done.4.rest_1_), custom_call_target="tpu_custom_call" | custom-call | flops 2097152 | bytes 6291456 | tf_op jit(solution)/shard_map/refresh/pallas_call | solution.py:221
  81.0 2.7 %convolution_convert_fusion.4 = bf16[128,512]{1,0:T(8,128)(2,1)S(1)} fusion(bf16[128,2048]{1,0:T(8,128)(2,1)} %collective-permute-done.2.rest_3_, bf16[512,2048]{1,0:T(8,128)(2,1)} %refresh.1), kind=kOutput, calls=%fused_computation.5 | convolution fusion | flops 268500992 | bytes 2752512 | tf_op jit(solution)/shard_map/dot_general | solution.py:269
  83.7 3.4 %collective-permute-start.7 = (bf16[128,512]{1,0:T(8,128)(2,1)S(1)}, bf16[128,512]{1,0:T(8,128)(2,1)S(1)}, u32[]{:S(2)}, u32[]{:S(2)}) collective-permute-start(bf16[128,512]{1,0:T(8,128)(2,1)S(1)} %convolution_convert_fusion.4), channel_id=1, source_target_pairs={{3,0},{2,1},{1,2},{0,3},{7,4},{6,5},{5,6},{4,7},{11,8},{10,9},{9,1... | collective-permute-start | bytes 393224 | tf_op jit(solution)/shard_map/ppermute | solution.py:44
  87.2 1.9 %convolution_convert_fusion.5 = bf16[128,512]{1,0:T(8,128)(2,1)S(1)} fusion(bf16[128,2048]{1,0:T(8,128)(2,1)} %collective-permute-done.1.rest_2_, bf16[512,2048]{1,0:T(8,128)(2,1)S(1)} %copy-done.1), kind=kOutput, calls=%fused_computation.6 | convolution fusion | flops 268500992 | bytes 2752512 | tf_op jit(solution)/shard_map/dot_general | solution.py:269
  89.2 1.9 %convolution_convert_fusion.6 = bf16[128,512]{1,0:T(8,128)(2,1)S(1)} fusion(bf16[128,2048]{1,0:T(8,128)(2,1)} %collective-permute-done.rest_0_.rest_1_, bf16[512,2048]{1,0:T(8,128)(2,1)S(1)} %copy-done.1), kind=kOutput, calls=%fused_computation.7 | convolution fusion | flops 268500992 | bytes 2752512 | tf_op jit(solution)/shard_map/dot_general | solution.py:269
  94.3 2.0 %collective-permute-start.8 = (bf16[128,512]{1,0:T(8,128)(2,1)S(1)}, bf16[128,512]{1,0:T(8,128)(2,1)S(1)}, u32[]{:S(2)}, u32[]{:S(2)}) collective-permute-start(bf16[128,512]{1,0:T(8,128)(2,1)S(1)} %convolution_convert_fusion.3), channel_id=1, source_target_pairs={{4,0},{5,1},{6,2},{7,3},{0,4},{1,5},{2,6},{3,7},{12,8},{13,9},{14,... | collective-permute-start | bytes 393224 | tf_op jit(solution)/shard_map/ppermute | solution.py:44
  96.3 1.9 %convolution_convert_fusion.1 = bf16[128,512]{1,0:T(8,128)(2,1)S(1)} fusion(bf16[128,2048]{1,0:T(8,128)(2,1)} %collective-permute-done.10, bf16[512,2048]{1,0:T(8,128)(2,1)S(1)} %copy-done.1), kind=kOutput, calls=%fused_computation.2 | convolution fusion | flops 268500992 | bytes 2752512 | tf_op jit(solution)/shard_map/dot_general | solution.py:269
  98.2 11.3 %collective-permute-done.12 = bf16[128,2048]{1,0:T(8,128)(2,1)} collective-permute-done((bf16[128,2048]{1,0:T(8,128)(2,1)}, bf16[128,2048]{1,0:T(8,128)(2,1)}, u32[]{:S(2)}, u32[]{:S(2)}) %collective-permute-start.12) | collective-permute-done | bytes 524320 | tf_op jit(solution)/shard_map/ppermute | solution.py:40
  110.0 1.9 %convolution_convert_fusion = bf16[128,512]{1,0:T(8,128)(2,1)S(1)} fusion(bf16[128,2048]{1,0:T(8,128)(2,1)} %collective-permute-done.12, bf16[512,2048]{1,0:T(8,128)(2,1)S(1)} %copy-done.1), kind=kOutput, calls=%fused_computation.1 | convolution fusion | flops 268500992 | bytes 2752512 | tf_op jit(solution)/shard_map/dot_general | solution.py:269
  112.0 1.6 %collective-permute-start.13 = (bf16[128,512]{1,0:T(8,128)(2,1)S(1)}, bf16[128,512]{1,0:T(8,128)(2,1)S(1)}, u32[]{:S(2)}, u32[]{:S(2)}) collective-permute-start(bf16[128,512]{1,0:T(8,128)(2,1)S(1)} %convolution_convert_fusion), channel_id=1, source_target_pairs={{7,0},{6,1},{5,2},{4,3},{3,4},{2,5},{1,6},{0,7},{15,8},{14,9},{13,... | collective-permute-start | bytes 393224 | tf_op jit(solution)/shard_map/ppermute | solution.py:44
  113.7 7.7 %collective-permute-done.9 = bf16[128,512]{1,0:T(8,128)(2,1)S(1)} collective-permute-done((bf16[128,512]{1,0:T(8,128)(2,1)S(1)}, bf16[128,512]{1,0:T(8,128)(2,1)S(1)}, u32[]{:S(2)}, u32[]{:S(2)}) %collective-permute-start.9) | collective-permute-done | bytes 131104 | tf_op jit(solution)/shard_map/ppermute | solution.py:44
  122.2 4.0 %collective-permute-done.13 = bf16[128,512]{1,0:T(8,128)(2,1)S(1)} collective-permute-done((bf16[128,512]{1,0:T(8,128)(2,1)S(1)}, bf16[128,512]{1,0:T(8,128)(2,1)S(1)}, u32[]{:S(2)}, u32[]{:S(2)}) %collective-permute-start.13) | collective-permute-done | bytes 131104 | tf_op jit(solution)/shard_map/ppermute | solution.py:44
  (46 shorter events, 13.0 us)
Async XLA Ops:
  4.9 29.3 %all-to-all-start = ((bf16[4,128,2048]{2,1,0:T(8,128)(2,1)}), bf16[4,128,2048]{2,1,0:T(8,128)(2,1)S(1)}, u32[]{:S(2)}, u32[]{:S(2)}) async-start(bf16[4,128,2048]{2,1,0:T(8,128)(2,1)} %get-tuple-element.12), calls=%async_computation | async-start | bytes 4194304 | tf_op jit(solution)/shard_map/all_to_all | solution.py:257
  8.5 68.9 %collective-permute-start.3 = (bf16[128,2048]{1,0:T(8,128)(2,1)}, bf16[128,2048]{1,0:T(8,128)(2,1)S(1)}, u32[]{:S(2)}, u32[]{:S(2)}) collective-permute-start(bf16[128,2048]{1,0:T(8,128)(2,1)} %get-tuple-element.13.rest_0_), channel_id=1, source_target_pairs={{0,4},{1,5},{2,6},{3,7},{4,0},{5,1},{6,2},{7,3},{8,12},{9,13},{10,... | collective-permute-start | bytes 1572872 | tf_op jit(solution)/shard_map/ppermute | solution.py:40
  11.8 32.4 %collective-permute-start = (bf16[128,2048]{1,0:T(8,128)(2,1)}, bf16[128,2048]{1,0:T(8,128)(2,1)}, u32[]{:S(2)}, u32[]{:S(2)}) collective-permute-start(bf16[128,2048]{1,0:T(8,128)(2,1)} %get-tuple-element.14), channel_id=1, source_target_pairs={{0,1},{1,0},{2,3},{3,2},{4,5},{5,4},{6,7},{7,6},{8,9},{9,8},{10,11... | collective-permute-start | bytes 1572872 | tf_op jit(solution)/shard_map/ppermute | solution.py:40
  13.7 35.1 %collective-permute-start.1 = (bf16[128,2048]{1,0:T(8,128)(2,1)}, bf16[128,2048]{1,0:T(8,128)(2,1)}, u32[]{:S(2)}, u32[]{:S(2)}) collective-permute-start(bf16[128,2048]{1,0:T(8,128)(2,1)} %get-tuple-element.16), channel_id=1, source_target_pairs={{0,2},{1,3},{2,0},{3,1},{4,6},{5,7},{6,4},{7,5},{8,10},{9,11},{10,... | collective-permute-start | bytes 1572872 | tf_op jit(solution)/shard_map/ppermute | solution.py:40
  15.3 45.2 %collective-permute-start.2 = (bf16[128,2048]{1,0:T(8,128)(2,1)}, bf16[128,2048]{1,0:T(8,128)(2,1)}, u32[]{:S(2)}, u32[]{:S(2)}) collective-permute-start(bf16[128,2048]{1,0:T(8,128)(2,1)} %get-tuple-element.17), channel_id=1, source_target_pairs={{0,3},{1,2},{2,1},{3,0},{4,7},{5,6},{6,5},{7,4},{8,11},{9,10},{10,... | collective-permute-start | bytes 1572872 | tf_op jit(solution)/shard_map/ppermute | solution.py:40
  15.4 62.1 %collective-permute-start.4 = (bf16[128,2048]{1,0:T(8,128)(2,1)}, bf16[128,2048]{1,0:T(8,128)(2,1)S(1)}, u32[]{:S(2)}, u32[]{:S(2)}) collective-permute-start(bf16[128,2048]{1,0:T(8,128)(2,1)} %get-tuple-element.18), channel_id=1, source_target_pairs={{0,6},{1,7},{2,4},{3,5},{4,2},{5,3},{6,0},{7,1},{8,14},{9,15},{10,... | collective-permute-start | bytes 1572872 | tf_op jit(solution)/shard_map/ppermute | solution.py:40
  34.2 1.3 %copy-start.2 = (bf16[4,128,2048]{2,1,0:T(8,128)(2,1)}, bf16[4,128,2048]{2,1,0:T(8,128)(2,1)S(1)}, u32[]{:S(2)}) copy-start(bf16[4,128,2048]{2,1,0:T(8,128)(2,1)S(1)} %all-to-all-done.rest_0_) | copy-start | bytes 6291460
  39.8 3.7 %copy-start.4 = (s32[7]{0:T(128)S(1)}, s32[7]{0:T(128)}, u32[]{:S(2)}) copy-start(s32[7]{0:T(128)} %named_ref.5) | copy-start | bytes 88
  39.8 3.7 %copy-start.5 = (s32[8]{0:T(128)S(1)}, s32[8]{0:T(128)}, u32[]{:S(2)}) copy-start(s32[8]{0:T(128)} %constant.27.clone) | copy-start | bytes 100
  39.8 37.6 %all-to-all-start.1 = ((bf16[4,128,2048]{2,1,0:T(8,128)(2,1)}), bf16[4,128,2048]{2,1,0:T(8,128)(2,1)S(1)}, u32[]{:S(2)}, u32[]{:S(2)}) async-start(bf16[4,128,2048]{2,1,0:T(8,128)(2,1)} %by_owner.1), calls=%async_computation.1 | async-start | bytes 4194304 | tf_op jit(solution)/shard_map/all_to_all | solution.py:264
  47.5 46.9 %collective-permute-start.10 = (bf16[128,2048]{1,0:T(8,128)(2,1)}, bf16[128,2048]{1,0:T(8,128)(2,1)}, u32[]{:S(2)}, u32[]{:S(2)}) collective-permute-start(bf16[128,2048]{1,0:T(8,128)(2,1)} %get-tuple-element.15.rest_0_), channel_id=1, source_target_pairs={{0,5},{1,4},{2,7},{3,6},{4,1},{5,0},{6,3},{7,2},{8,13},{9,12},{10,... | collective-permute-start | bytes 1572872 | tf_op jit(solution)/shard_map/ppermute | solution.py:40
  48.8 60.7 %collective-permute-start.12 = (bf16[128,2048]{1,0:T(8,128)(2,1)}, bf16[128,2048]{1,0:T(8,128)(2,1)}, u32[]{:S(2)}, u32[]{:S(2)}) collective-permute-start(bf16[128,2048]{1,0:T(8,128)(2,1)} %get-tuple-element.20), channel_id=1, source_target_pairs={{0,7},{1,6},{2,5},{3,4},{4,3},{5,2},{6,1},{7,0},{8,15},{9,14},{10,... | collective-permute-start | bytes 1572872 | tf_op jit(solution)/shard_map/ppermute | solution.py:40
  77.5 1.6 %copy-start = (bf16[512,2048]{1,0:T(8,128)(2,1)S(1)}, bf16[512,2048]{1,0:T(8,128)(2,1)}, u32[]{:S(2)}) copy-start(bf16[512,2048]{1,0:T(8,128)(2,1)} %newton.1.update_ref) | copy-start | bytes 6291460
  81.0 6.2 %copy-start.1 = (bf16[512,2048]{1,0:T(8,128)(2,1)S(1)}, bf16[512,2048]{1,0:T(8,128)(2,1)}, u32[]{:S(2)}) copy-start(bf16[512,2048]{1,0:T(8,128)(2,1)} %refresh.1) | copy-start | bytes 6291460
  83.7 8.0 %copy-start.3 = (bf16[128,2048]{1,0:T(8,128)(2,1)S(1)}, bf16[128,2048]{1,0:T(8,128)(2,1)}, u32[]{:S(2)}) copy-start(bf16[128,2048]{1,0:T(8,128)(2,1)} %get-tuple-element.19) | copy-start | bytes 1572868
  83.7 29.9 %collective-permute-start.7 = (bf16[128,512]{1,0:T(8,128)(2,1)S(1)}, bf16[128,512]{1,0:T(8,128)(2,1)S(1)}, u32[]{:S(2)}, u32[]{:S(2)}) collective-permute-start(bf16[128,512]{1,0:T(8,128)(2,1)S(1)} %convolution_convert_fusion.4), channel_id=1, source_target_pairs={{3,0},{2,1},{1,2},{0,3},{7,4},{6,5},{5,6},{4,7},{11,8},{10,9},{9,1... | collective-permute-start | bytes 393224 | tf_op jit(solution)/shard_map/ppermute | solution.py:44
  89.1 22.9 %collective-permute-start.6 = (bf16[128,512]{1,0:T(8,128)(2,1)S(1)}, bf16[128,512]{1,0:T(8,128)(2,1)S(1)}, u32[]{:S(2)}, u32[]{:S(2)}) collective-permute-start(bf16[128,512]{1,0:T(8,128)(2,1)S(1)} %convolution_convert_fusion.5), channel_id=1, source_target_pairs={{2,0},{3,1},{0,2},{1,3},{6,4},{7,5},{4,6},{5,7},{10,8},{11,9},{8,1... | collective-permute-start | bytes 393224 | tf_op jit(solution)/shard_map/ppermute | solution.py:44
  91.1 20.8 %collective-permute-start.5 = (bf16[128,512]{1,0:T(8,128)(2,1)S(1)}, bf16[128,512]{1,0:T(8,128)(2,1)S(1)}, u32[]{:S(2)}, u32[]{:S(2)}) collective-permute-start(bf16[128,512]{1,0:T(8,128)(2,1)S(1)} %convolution_convert_fusion.6), channel_id=1, source_target_pairs={{1,0},{0,1},{3,2},{2,3},{5,4},{4,5},{7,6},{6,7},{9,8},{8,9},{11,10... | collective-permute-start | bytes 393224 | tf_op jit(solution)/shard_map/ppermute | solution.py:44
  94.3 19.3 %collective-permute-start.8 = (bf16[128,512]{1,0:T(8,128)(2,1)S(1)}, bf16[128,512]{1,0:T(8,128)(2,1)S(1)}, u32[]{:S(2)}, u32[]{:S(2)}) collective-permute-start(bf16[128,512]{1,0:T(8,128)(2,1)S(1)} %convolution_convert_fusion.3), channel_id=1, source_target_pairs={{4,0},{5,1},{6,2},{7,3},{0,4},{1,5},{2,6},{3,7},{12,8},{13,9},{14,... | collective-permute-start | bytes 393224 | tf_op jit(solution)/shard_map/ppermute | solution.py:44
  109.5 11.9 %collective-permute-start.9 = (bf16[128,512]{1,0:T(8,128)(2,1)S(1)}, bf16[128,512]{1,0:T(8,128)(2,1)S(1)}, u32[]{:S(2)}, u32[]{:S(2)}) collective-permute-start(bf16[128,512]{1,0:T(8,128)(2,1)S(1)} %convolution_convert_fusion.2), channel_id=1, source_target_pairs={{6,0},{7,1},{4,2},{5,3},{2,4},{3,5},{0,6},{1,7},{14,8},{15,9},{12,... | collective-permute-start | bytes 393224 | tf_op jit(solution)/shard_map/ppermute | solution.py:44
  111.9 10.3 %collective-permute-start.11 = (bf16[128,512]{1,0:T(8,128)(2,1)S(1)}, bf16[128,512]{1,0:T(8,128)(2,1)S(1)}, u32[]{:S(2)}, u32[]{:S(2)}) collective-permute-start(bf16[128,512]{1,0:T(8,128)(2,1)S(1)} %convolution_convert_fusion.1), channel_id=1, source_target_pairs={{5,0},{4,1},{7,2},{6,3},{1,4},{0,5},{3,6},{2,7},{13,8},{12,9},{15,... | collective-permute-start | bytes 393224 | tf_op jit(solution)/shard_map/ppermute | solution.py:44
  112.0 14.3 %collective-permute-start.13 = (bf16[128,512]{1,0:T(8,128)(2,1)S(1)}, bf16[128,512]{1,0:T(8,128)(2,1)S(1)}, u32[]{:S(2)}, u32[]{:S(2)}) collective-permute-start(bf16[128,512]{1,0:T(8,128)(2,1)S(1)} %convolution_convert_fusion), channel_id=1, source_target_pairs={{7,0},{6,1},{5,2},{4,3},{3,4},{2,5},{1,6},{0,7},{15,8},{14,9},{13,... | collective-permute-start | bytes 393224 | tf_op jit(solution)/shard_map/ppermute | solution.py:44

commit v3 on v2

v3 whole, which is shorter than its diff:
```python
import functools
import math

import jax
import jax.numpy as jnp
from jax import lax
from jax.experimental import pallas as pl
from jax.experimental.pallas import tpu as pltpu
from jax.sharding import PartitionSpec as P

ITERS = 4


quintic_one = 3.4445
quintic_two = -4.775
quintic_three = 2.0315
learn_rate = 0.05
weight_decay = 0.1
norm_eps = 1e-07

ROW_BY_ROW = (((1,), (1,)), ((), ()))
ANY = pl.BlockSpec(memory_space=pl.ANY)
SMEM = pl.BlockSpec(memory_space=pltpu.SMEM)
VMEM = pl.BlockSpec(memory_space=pltpu.VMEM)


def partner(index, step, size):
    if size & (size - 1) == 0:
        return index ^ step
    return (index + step) % size


def source(index, step, size):
    if size & (size - 1) == 0:
        return index ^ step
    return (index + size - step) % size


def send(value, axis, step, size):
    return lax.ppermute(value, axis, [(i, partner(i, step, size)) for i in range(size)])


def send_back(value, axis, step, size):
    return lax.ppermute(value, axis, [(partner(i, step, size), i) for i in range(size)])


def after(value, *others):
    return lax.optimization_barrier((value, *others))[0]


def block_of(group, named_ref, blocks, owners):
    slot = jnp.int32(0)
    for b in range(blocks):
        slot = jnp.where(lax.div(named_ref[b], jnp.int32(owners)) == group, b, slot)
    return slot


def pick_kernel(wanted, owners, tokens_ref, named_ref, *rest):
    outs, sem = rest[-1 - len(wanted) : -1], rest[-1]
    if rest[-2].ndim == 3:
        outs = [rest[-2].at[k] for k in range(len(wanted))]
    copies = []
    for k, group_of in enumerate(wanted):
        slot = block_of(group_of(), named_ref, tokens_ref.shape[0], owners)
        copies.append(pltpu.make_async_copy(tokens_ref.at[slot], outs[k], sem.at[k]))
        copies[-1].start()
    for copy in copies:
        copy.wait()


def pick(resident, named, wanted, owners, stacked, *later_than):
    shape = resident.shape[1:]
    size = math.prod(shape) * resident.dtype.itemsize * len(wanted)
    if stacked:
        out_shape = jax.ShapeDtypeStruct((len(wanted),) + shape, resident.dtype)
    else:
        out_shape = [jax.ShapeDtypeStruct(shape, resident.dtype)] * len(wanted)
    return pl.pallas_call(
        functools.partial(pick_kernel, wanted, owners),
        out_shape=out_shape,
        in_specs=[ANY, SMEM] + [ANY] * len(later_than),
        out_specs=VMEM if stacked else [VMEM] * len(wanted),
        scratch_shapes=[pltpu.SemaphoreType.DMA((len(wanted),))],
        compiler_params=pltpu.CompilerParams(vmem_limit_bytes=56 << 20),
        cost_estimate=pl.CostEstimate(flops=0, bytes_accessed=2 * size, transcendentals=0),
        name="pick",
    )(resident, named, *later_than)


def by_owner_kernel(owners, scale, later, array_ref, owner_ref, *rest):
    outs, scratch = rest[later : later + owners], rest[later + owners :]
    held, sem = (outs, scratch[0]) if scale is None else scratch
    first = lax.axis_index("replica") * owners
    column = lax.axis_index("fsdp")
    copies = []
    for k in range(owners):
        expert = owner_ref[first + partner(column, k, owners)] - first
        target = outs[k] if scale is None else held.at[k]
        copies.append(pltpu.make_async_copy(array_ref.at[expert], target, sem.at[k]))
    for copy in copies:
        copy.start()
    for k, copy in enumerate(copies):
        copy.wait()
        if scale is not None:
            outs[k][...] = (held[k] * scale).astype(outs[k].dtype)


def by_owner(array, owner_expert, scale, *later_than):
    owners = array.shape[0]
    scratch = [pltpu.SemaphoreType.DMA((owners,))]
    if scale is not None:
        scratch = [pltpu.VMEM(array.shape, array.dtype)] + scratch
    return pl.pallas_call(
        functools.partial(by_owner_kernel, owners, scale, len(later_than)),
        out_shape=[jax.ShapeDtypeStruct(array.shape[1:], jnp.bfloat16)] * owners,
        in_specs=[ANY, SMEM] + [ANY] * len(later_than),
        out_specs=[VMEM] * owners,
        scratch_shapes=scratch,
        compiler_params=pltpu.CompilerParams(vmem_limit_bytes=56 << 20),
        cost_estimate=pl.CostEstimate(
            flops=0, bytes_accessed=array.size * (array.dtype.itemsize + 2), transcendentals=0
        ),
        name="by_owner",
    )(array, owner_expert, *later_than)


def newton_kernel(chunk, owners, *rest):
    pieces, (out_ref, poly_ref) = rest[:owners], rest[-2:]
    shard, width = pieces[0].shape
    column = lax.axis_index("fsdp")
    total = jnp.float32(0.0)
    for piece in pieces:
        wide = piece[...].astype(jnp.float32)
        total += jnp.sum(wide * wide)
    scale = 1.0 / (jnp.sqrt(total) + norm_eps)
    for step, piece in enumerate(pieces):
        start = source(column, step, owners) * shard
        out_ref[pl.ds(pl.multiple_of(start, shard), shard), :] = (
            piece[...].astype(jnp.float32) * scale
        ).astype(jnp.bfloat16)

    def iteration(_, carry):
        state = out_ref[...]
        square = lax.dot_general(
            state, state, ROW_BY_ROW, preferred_element_type=jnp.float32
        ).astype(jnp.bfloat16)
        twice = jnp.dot(square, square, preferred_element_type=jnp.float32)
        poly_ref[...] = (
            quintic_two * square.astype(jnp.float32) + quintic_three * twice
        ).astype(jnp.bfloat16)

        def columns(c, carry):
            at = pl.ds(pl.multiple_of(c * chunk, chunk), chunk)
            part = out_ref[:, at]
            out_ref[:, at] = (
                quintic_one * part.astype(jnp.float32)
                + jnp.dot(poly_ref[...], part, preferred_element_type=jnp.float32)
            ).astype(jnp.bfloat16)
            return carry

        return lax.fori_loop(0, width // chunk, columns, carry)

    lax.fori_loop(0, ITERS, iteration, 0)


def orthogonalize(pieces, *later_than):
    owners = len(pieces)
    rows, width = pieces[0].shape[0] * owners, pieces[0].shape[1]
    chunk = 1024 if width % 1024 == 0 else width
    return pl.pallas_call(
        functools.partial(newton_kernel, chunk, owners),
        out_shape=jax.ShapeDtypeStruct((rows, width), jnp.bfloat16),
        in_specs=[VMEM] * owners + [ANY] * len(later_than),
        out_specs=VMEM,
        scratch_shapes=[pltpu.VMEM((rows, rows), jnp.bfloat16)],
        compiler_params=pltpu.CompilerParams(vmem_limit_bytes=56 << 20),
        cost_estimate=pl.CostEstimate(
            flops=ITERS * 2 * rows * rows * (2 * width + rows),
            bytes_accessed=4 * rows * width,
            transcendentals=0,
        ),
        name="newton",
    )(*pieces, *later_than)


def refresh_kernel(factor, owners, update_ref, *rest):
    pieces, out_ref = rest[:owners], rest[-1]
    shard = pieces[0].shape[0]
    column = lax.axis_index("fsdp")
    for step, piece in enumerate(pieces):
        at = pl.ds(pl.multiple_of(source(column, step, owners) * shard, shard), shard)
        out_ref[at, :] = (
            piece[...].astype(jnp.float32) - factor * update_ref[at, :].astype(jnp.float32)
        ).astype(jnp.bfloat16)


def refresh(update, pieces, *later_than):
    factor = learn_rate * 0.2 * math.sqrt(max(update.shape))
    return pl.pallas_call(
        functools.partial(refresh_kernel, factor, len(pieces)),
        out_shape=jax.ShapeDtypeStruct(update.shape, jnp.bfloat16),
        in_specs=[VMEM] * (1 + len(pieces)) + [ANY] * len(later_than),
        out_specs=VMEM,
        compiler_params=pltpu.CompilerParams(vmem_limit_bytes=32 << 20),
        cost_estimate=pl.CostEstimate(
            flops=2 * update.size, bytes_accessed=6 * update.size, transcendentals=0
        ),
        name="refresh",
    )(update, *pieces, *later_than)


def per_device(weights, momentum, tokens, block_expert, owner_expert):
    owners = lax.axis_size("fsdp")
    groups = lax.axis_size("replica")
    group = lax.axis_index("replica")
    blocks = block_expert.shape[0]
    width = tokens.shape[1]
    rows = weights.shape[1] * owners
    resident = tokens.reshape(blocks, -1, width)
    half = groups // 2
    places = list(range(0, groups, 2))
    teams = [[team + place for place in places] for team in (0, 1)]
    far = list(range(half + 1, groups, 2))
    near = list(range(1, half, 2))

    def at_step(step):
        return lambda: partner(lax.axis_index("replica"), step, groups)

    def at_place(place):
        return lambda: lax.axis_index("replica") % 2 + place

    arrived = {}

    def pick_and_send(steps, *later_than):
        picked = pick(
            resident, block_expert, [at_step(step) for step in steps], owners, False, *later_than
        )
        for block, step in zip(picked, steps):
            arrived[step] = send(block, "replica", step, groups)
        return picked

    def exchange(blocks):
        return lax.all_to_all(blocks, "replica", 0, 0, axis_index_groups=teams, tiled=True)

    outgoing = pick(resident, block_expert, [at_place(place) for place in places], owners, True)
    team = exchange(outgoing)
    moment = by_owner(momentum, owner_expert, None, outgoing)
    moment = [moment[0]] + [send(moment[k], "fsdp", k, owners) for k in range(1, owners)]
    pick_and_send(near, outgoing)
    sent = pick_and_send(far, *moment, arrived[near[0]])
    kept = 1.0 - learn_rate * weight_decay
    master = by_owner(weights, owner_expert, kept, *moment )
    master = [master[0]] + [send(master[k], "fsdp", k, owners) for k in range(1, owners)]
    update = orthogonalize(moment , *[arrived[step] for step in near], sent[0])
    refreshed = refresh(update, master )

    def product(block):
        return lax.dot_general(
            block, refreshed, ROW_BY_ROW, preferred_element_type=jnp.float32
        ).astype(jnp.bfloat16)

    reply = product(team.reshape(-1, width)).reshape(half, -1, rows)
    answers = [exchange(reply)]
    steps = near + far
    replies = []
    for step in steps:
        replies.append(product(after(arrived[step], reply, *replies)))
        answers.append(send_back(replies[-1], "replica", step, groups)[None])
    served = jnp.concatenate(
        [
            group % 2 + jnp.array(places, jnp.int32),
            partner(group, jnp.array(steps, jnp.int32), groups),
        ]
    )
    order = jnp.argmax((block_expert // owners)[:, None] == served[None, :], axis=1)
    rollout = jnp.take(jnp.concatenate(answers), order, axis=0, mode="clip").reshape(-1, rows)
    return (refreshed[None], rollout)


def solution(mesh):
    placed = (
        P("replica", "fsdp", None),
        P("replica", "fsdp", None),
        P(("fsdp", "replica"), None),
        P(("fsdp", "replica")),
        P(),
    )
    return jax.shard_map(
        per_device,
        mesh=mesh,
        in_specs=placed,
        out_specs=(P(("fsdp", "replica"), None, None), P(("fsdp", "replica"), None)),
        check_vma=False,
    )
```

time: 129 us -> 128 us (level); the launches traced: 128 us -> 125 us
  matrix products: 12.9 us -> 9.87 us
  Pallas kernels: 33.8 us -> 35.6 us
  starting transfers between devices: 26.2 us -> 24.4 us
    ppermute x7 -> x10, waiting for transfers between devices: 20.4 us -> 41.4 us  [send(): lax.ppermute(value, axis, [(i, partner(i, step, size)) for i in range(siz...]
    all_to_all x2, waiting for transfers between devices: 15.8 us -> 0.3 us  [exchange(): lax.all_to_all(blocks, 'replica', 0, 0, axis_index_groups=teams, tiled=True)]
    ppermute x7 -> x4, waiting for transfers between devices: 12.6 us -> 6.61 us  [send_back(): lax.ppermute(value, axis, [(partner(i, step, size), i) for i in range(siz...]
    pallas_call x1 -> x2, Pallas kernels: 4.29 us -> 7.92 us  [by_owner(): pl.pallas_call(functools.partial(by_owner_kernel, owners, scale, len(late...]
    dot_general x8 -> x5, matrix products: 12.9 us -> 9.87 us  [product(): lax.dot_general(block, refreshed, ROW_BY_ROW, preferred_element_type=jnp....]
    ppermute x7 -> x10, starting transfers between devices: 10.7 us -> 8.08 us  [send(): lax.ppermute(value, axis, [(i, partner(i, step, size)) for i in range(siz...]
    all_to_all x2, starting transfers between devices: 7.24 us -> 9.41 us  [exchange(): lax.all_to_all(blocks, 'replica', 0, 0, axis_index_groups=teams, tiled=True)]
    pallas_call x5, Pallas kernels: 29.5 us -> 27.7 us  [the longest x1 16.4 us: orthogonalize(): pl.pallas_call(functools.partial(newton_kernel, chunk, owners), out_shape...]
  transfers between devices with their start and end apart: 16 -> 16, of which waited for: 6 -> 7; matrix products, arithmetic and copies ran while one was open for 11% -> 9% of each run, Pallas kernels for 23% -> 26%
where the time goes in v3:
time: 128 us; the launch traced here: 125 us
  waiting for transfers between devices  48.3 us (38%)
  Pallas kernels  35.6 us (28%)
  starting transfers between devices  24.4 us (19%)
  matrix products  9.87 us (8%)
  local copies, waits for them, and re-layouts  5.65 us (4%)
    ppermute x10, waiting for transfers between devices, send(): lax.ppermute(value, axis, [(i, partner(i, step, size)) for i in range(siz...  41.4 us
    pallas_call x1, Pallas kernels, orthogonalize(): pl.pallas_call(functools.partial(newton_kernel, chunk, owners), out_shape...  16.4 us
    dot_general x5, matrix products, product(): lax.dot_general(block, refreshed, ROW_BY_ROW, preferred_element_type=jnp....  9.87 us
    all_to_all x2, starting transfers between devices, exchange(): lax.all_to_all(blocks, 'replica', 0, 0, axis_index_groups=teams, tiled=True)  9.41 us
    pallas_call x3, Pallas kernels, pick(): pl.pallas_call(functools.partial(pick_kernel, wanted, owners), out_shape=...  9.29 us
    ppermute x10, starting transfers between devices, send(): lax.ppermute(value, axis, [(i, partner(i, step, size)) for i in range(siz...  8.08 us
    pallas_call x2, Pallas kernels, by_owner(): pl.pallas_call(functools.partial(by_owner_kernel, owners, scale, len(late...  7.92 us
    ppermute x4, starting transfers between devices, send_back(): lax.ppermute(value, axis, [(partner(i, step, size), i) for i in range(siz...  6.93 us
  transfers between devices with their start and end apart: 16, of which 7 were waited for; matrix products, arithmetic and copies ran while one was open for 9% of the time, Pallas kernels for 26%

profile of v3, /device:TPU:16, one launch (start us, length us, event | category | flops | bytes accessed | tf_op | source)
XLA Modules:
  0.0 125.5 jit_solution(12526987394615134692)
XLA Ops:
  0.6 3.5 %pick.3.rest_0_ = bf16[4,128,2048]{2,1,0:T(8,128)(2,1)} custom-call(bf16[7,128,2048]{2,1,0:T(8,128)(2,1)} %bitcast.24, s32[7]{0:T(128)} %named_ref.5), custom_call_target="tpu_custom_call" | custom-call | bytes 4194304 | tf_op jit(solution)/shard_map/pick/pallas_call | solution.py:78
  4.2 5.2 %all-to-all-start = ((bf16[4,128,2048]{2,1,0:T(8,128)(2,1)}), bf16[4,128,2048]{2,1,0:T(8,128)(2,1)}, u32[]{:S(2)}, u32[]{:S(2)}) async-start(bf16[4,128,2048]{2,1,0:T(8,128)(2,1)} %pick.3.rest_0_), calls=%async_computation | async-start | bytes 4194304 | tf_op jit(solution)/shard_map/all_to_all | solution.py:243
  9.4 3.6 %by_owner.2 = (bf16[128,2048]{1,0:T(8,128)(2,1)}, bf16[128,2048]{1,0:T(8,128)(2,1)}, bf16[128,2048]{1,0:T(8,128)(2,1)}, bf16[128,2048]{1,0:T(8,128)(2,1)}) custom-call(bf16[4,128,2048]{2,1,0:T(8,128)(2,1)} %array_ref.2, s32[32]{0:T(128)} %owner_ref.3, bf16[4,128,2048]{2,1,0:T(8,128)(2,1)} %pick.3.rest_0_), custom_call_target="tpu_custom_call" | custom-call | bytes 4194304 | tf_op jit(solution)/shard_map/by_owner/pallas_call | solution.py:113
  13.0 1.6 %collective-permute-start.1 = (bf16[128,2048]{1,0:T(8,128)(2,1)}, bf16[128,2048]{1,0:T(8,128)(2,1)S(1)}, u32[]{:S(2)}, u32[]{:S(2)}) collective-permute-start(bf16[128,2048]{1,0:T(8,128)(2,1)} %get-tuple-element.21), channel_id=1, source_target_pairs={{0,16},{8,24},{16,0},{24,8},{1,17},{9,25},{17,1},{25,9},{2,18},{10... | collective-permute-start | bytes 1572872 | tf_op jit(solution)/shard_map/ppermute | solution.py:40
  14.9 2.9 %pick.4 = (bf16[128,2048]{1,0:T(8,128)(2,1)}, bf16[128,2048]{1,0:T(8,128)(2,1)}) custom-call(bf16[7,128,2048]{2,1,0:T(8,128)(2,1)} %bitcast.25, s32[7]{0:T(128)} %named_ref.5, bf16[4,128,2048]{2,1,0:T(8,128)(2,1)} %pick.3.rest_0_), custom_call_target="tpu_custom_call" | custom-call | bytes 2097152 | tf_op jit(solution)/shard_map/pick/pallas_call | solution.py:78
  17.8 1.6 %collective-permute-start.3 = (bf16[128,2048]{1,0:T(8,128)(2,1)}, bf16[128,2048]{1,0:T(8,128)(2,1)S(1)}, u32[]{:S(2)}, u32[]{:S(2)}) collective-permute-start(bf16[128,2048]{1,0:T(8,128)(2,1)} %get-tuple-element.23), channel_id=1, source_target_pairs={{0,1},{1,0},{2,3},{3,2},{4,5},{5,4},{6,7},{7,6},{8,9},{9,8},{10,11... | collective-permute-start | bytes 1572872 | tf_op jit(solution)/shard_map/ppermute | solution.py:40
  21.7 6.4 %collective-permute-done.1.rest_2_ = bf16[128,2048]{1,0:T(8,128)(2,1)S(1)} collective-permute-done((bf16[128,2048]{1,0:T(8,128)(2,1)}, bf16[128,2048]{1,0:T(8,128)(2,1)S(1)}, u32[]{:S(2)}, u32[]{:S(2)}) %collective-permute-start.1) | collective-permute-done | bytes 524320 | tf_op jit(solution)/shard_map/ppermute | solution.py:40
  28.0 10.3 %collective-permute-done.2.rest_3_ = bf16[128,2048]{1,0:T(8,128)(2,1)S(1)} collective-permute-done((bf16[128,2048]{1,0:T(8,128)(2,1)}, bf16[128,2048]{1,0:T(8,128)(2,1)S(1)}, u32[]{:S(2)}, u32[]{:S(2)}) %collective-permute-start.2) | collective-permute-done | bytes 524320 | tf_op jit(solution)/shard_map/ppermute | solution.py:40
  39.2 4.4 %by_owner.3 = (bf16[128,2048]{1,0:T(8,128)(2,1)}, bf16[128,2048]{1,0:T(8,128)(2,1)}, bf16[128,2048]{1,0:T(8,128)(2,1)}, bf16[128,2048]{1,0:T(8,128)(2,1)}) custom-call(f32[4,128,2048]{2,1,0:T(8,128)} %array_ref.3, s32[32]{0:T(128)} %owner_ref.3, bf16[128,2048]{1,0:T(8,128)(2,1)} %get-tuple-element.19.rest_0_, bf16[128,2048]{1,0:T(8,128)(2,1)} %copy-done.3, ...), custom_call_target="tpu_custom_call" | custom-call | bytes 6291456 | tf_op jit(solution)/shard_map/by_owner/pallas_call | solution.py:113
  46.6 2.9 %pick.5 = (bf16[128,2048]{1,0:T(8,128)(2,1)}, bf16[128,2048]{1,0:T(8,128)(2,1)}) custom-call(bf16[7,128,2048]{2,1,0:T(8,128)(2,1)} %bitcast.26, s32[7]{0:T(128)} %named_ref.5, bf16[128,2048]{1,0:T(8,128)(2,1)} %get-tuple-element.19.rest_0_, bf16[128,2048]{1,0:T(8,128)(2,1)} %copy-done.3, bf16[128,2048]{1,0:T(8,128)(2,1)} %copy-done.4, ...), custom_call_target="tpu_custom_call" | custom-call | bytes 2097152 | tf_op jit(solution)/shard_map/pick/pallas_call | solution.py:78
  50.4 9.1 %collective-permute-done.4.rest_5_ = bf16[128,2048]{1,0:T(8,128)(2,1)S(1)} collective-permute-done((bf16[128,2048]{1,0:T(8,128)(2,1)}, bf16[128,2048]{1,0:T(8,128)(2,1)S(1)}, u32[]{:S(2)}, u32[]{:S(2)}) %collective-permute-start.4) | collective-permute-done | bytes 524320 | tf_op jit(solution)/shard_map/ppermute | solution.py:40
  60.3 16.4 %newton.1.update_ref = bf16[512,2048]{1,0:T(8,128)(2,1)} custom-call(bf16[128,2048]{1,0:T(8,128)(2,1)} %get-tuple-element.19.rest_0_, bf16[128,2048]{1,0:T(8,128)(2,1)} %copy-done.3, bf16[128,2048]{1,0:T(8,128)(2,1)} %copy-done.4, bf16[128,2048]{1,0:T(8,128)(2,1)} %copy-done.5, bf16[128,2048]{1,0:T(8,128)(2,1)} %copy-done.6, bf16[128,2048]{1,0:T(8,128)(2,1)} %copy-done.8, ...), custom_call_target="tpu_custom_call" | custom-call | flops 9663676416 | bytes 4194304 | tf_op jit(solution)/shard_map/newton/pallas_call | solution.py:170
  76.8 1.6 %copy-done = bf16[512,2048]{1,0:T(8,128)(2,1)S(1)} copy-done((bf16[512,2048]{1,0:T(8,128)(2,1)S(1)}, bf16[512,2048]{1,0:T(8,128)(2,1)}, u32[]{:S(2)}) %copy-start) | copy-done | bytes 2097176
  78.4 1.9 %refresh.1 = bf16[512,2048]{1,0:T(8,128)(2,1)} custom-call(bf16[512,2048]{1,0:T(8,128)(2,1)S(1)} %copy-done, bf16[128,2048]{1,0:T(8,128)(2,1)S(1)} %copy-done.1, bf16[128,2048]{1,0:T(8,128)(2,1)S(1)} %collective-permute-done.5.rest_1_, bf16[128,2048]{1,0:T(8,128)(2,1)S(1)} %collective-permute-done.6.rest_2_, bf16[128,2048]{1,0:T(8,128)(2,1)S(1)} %collective-permute-done.7.rest_3_), custom_call_target="tpu_custom_call" | custom-call | flops 2097152 | bytes 6291456 | tf_op jit(solution)/shard_map/refresh/pallas_call | solution.py:199
  80.3 4.5 %convolution_convert_fusion = bf16[512,512]{1,0:T(8,128)(2,1)} fusion(bf16[512,2048]{1,0:T(8,128)(2,1)} %bitcast.2, bf16[512,2048]{1,0:T(8,128)(2,1)} %refresh.1), kind=kOutput, calls=%fused_computation.1 | convolution fusion | flops 1074003968 | bytes 4718592 | tf_op jit(solution)/shard_map/dot_general | solution.py:258
  84.8 4.2 %all-to-all-start.1 = ((bf16[4,128,512]{2,1,0:T(8,128)(2,1)}), bf16[4,128,512]{2,1,0:T(8,128)(2,1)S(1)}, u32[]{:S(2)}, u32[]{:S(2)}) async-start(bf16[4,128,512]{2,1,0:T(8,128)(2,1)} %bitcast.28), calls=%async_computation.1 | async-start | bytes 1048576 | tf_op jit(solution)/shard_map/all_to_all | solution.py:243
  92.1 1.6 %collective-permute-start.9 = (bf16[128,512]{1,0:T(8,128)(2,1)S(1)}, bf16[128,512]{1,0:T(8,128)(2,1)S(1)}, u32[]{:S(2)}, u32[]{:S(2)}) collective-permute-start(bf16[128,512]{1,0:T(8,128)(2,1)S(1)} %convolution_convert_fusion.3), channel_id=1, source_target_pairs={{3,0},{2,1},{1,2},{0,3},{7,4},{6,5},{5,6},{4,7},{11,8},{10,9},{9,1... | collective-permute-start | bytes 393224 | tf_op jit(solution)/shard_map/ppermute | solution.py:44
  93.7 1.9 %convolution_convert_fusion.2 = bf16[128,512]{1,0:T(8,128)(2,1)S(1)} fusion(bf16[128,2048]{1,0:T(8,128)(2,1)} %collective-permute-done.10, bf16[512,2048]{1,0:T(8,128)(2,1)S(1)} %copy-done.2), kind=kOutput, calls=%fused_computation.3 | convolution fusion | flops 268500992 | bytes 2752512 | tf_op jit(solution)/shard_map/dot_general | solution.py:258
  95.6 3.1 %collective-permute-start.11 = (bf16[128,512]{1,0:T(8,128)(2,1)S(1)}, bf16[128,512]{1,0:T(8,128)(2,1)S(1)}, u32[]{:S(2)}, u32[]{:S(2)}) collective-permute-start(bf16[128,512]{1,0:T(8,128)(2,1)S(1)} %convolution_convert_fusion.2), channel_id=1, source_target_pairs={{5,0},{4,1},{7,2},{6,3},{1,4},{0,5},{3,6},{2,7},{13,8},{12,9},{15,... | collective-permute-start | bytes 393224 | tf_op jit(solution)/shard_map/ppermute | solution.py:44
  98.7 15.5 %collective-permute-done.12 = bf16[128,2048]{1,0:T(8,128)(2,1)} collective-permute-done((bf16[128,2048]{1,0:T(8,128)(2,1)}, bf16[128,2048]{1,0:T(8,128)(2,1)}, u32[]{:S(2)}, u32[]{:S(2)}) %collective-permute-start.12) | collective-permute-done | bytes 524320 | tf_op jit(solution)/shard_map/ppermute | solution.py:40
  114.3 1.9 %convolution_convert_fusion.1 = bf16[128,512]{1,0:T(8,128)(2,1)S(1)} fusion(bf16[128,2048]{1,0:T(8,128)(2,1)} %collective-permute-done.12, bf16[512,2048]{1,0:T(8,128)(2,1)S(1)} %copy-done.2), kind=kOutput, calls=%fused_computation.2 | convolution fusion | flops 268500992 | bytes 2752512 | tf_op jit(solution)/shard_map/dot_general | solution.py:258
  117.3 2.6 %collective-permute-done.11 = bf16[128,512]{1,0:T(8,128)(2,1)S(1)} collective-permute-done((bf16[128,512]{1,0:T(8,128)(2,1)S(1)}, bf16[128,512]{1,0:T(8,128)(2,1)S(1)}, u32[]{:S(2)}, u32[]{:S(2)}) %collective-permute-start.11) | collective-permute-done | bytes 131104 | tf_op jit(solution)/shard_map/ppermute | solution.py:44
  119.9 4.0 %collective-permute-done.13 = bf16[128,512]{1,0:T(8,128)(2,1)S(1)} collective-permute-done((bf16[128,512]{1,0:T(8,128)(2,1)S(1)}, bf16[128,512]{1,0:T(8,128)(2,1)S(1)}, u32[]{:S(2)}, u32[]{:S(2)}) %collective-permute-start.13) | collective-permute-done | bytes 131104 | tf_op jit(solution)/shard_map/ppermute | solution.py:44
  123.9 1.5 %gather_fusion = bf16[7,128,512]{2,1,0:T(8,128)(2,1)} fusion(bf16[8,128,512]{2,1,0:T(8,128)(2,1)S(1)} %bitcast_dynamic-update-slice_fusion, s32[1024]{0:T(1024)S(1)} %pad_clamp_fusion), kind=kCustom, calls=%fused_computation | custom fusion | bytes 1835036 | tf_op jit(solution)/shard_map/jit(_take)/gather | solution.py:276
  (55 shorter events, 12.5 us)
Async XLA Ops:
  4.2 76.1 %all-to-all-start = ((bf16[4,128,2048]{2,1,0:T(8,128)(2,1)}), bf16[4,128,2048]{2,1,0:T(8,128)(2,1)}, u32[]{:S(2)}, u32[]{:S(2)}) async-start(bf16[4,128,2048]{2,1,0:T(8,128)(2,1)} %pick.3.rest_0_), calls=%async_computation | async-start | bytes 4194304 | tf_op jit(solution)/shard_map/all_to_all | solution.py:243
  13.0 8.7 %collective-permute-start = (bf16[128,2048]{1,0:T(8,128)(2,1)}, bf16[128,2048]{1,0:T(8,128)(2,1)S(1)}, u32[]{:S(2)}, u32[]{:S(2)}) collective-permute-start(bf16[128,2048]{1,0:T(8,128)(2,1)} %get-tuple-element.20), channel_id=1, source_target_pairs={{0,8},{8,0},{16,24},{24,16},{1,9},{9,1},{17,25},{25,17},{2,10},{10... | collective-permute-start | bytes 1572872 | tf_op jit(solution)/shard_map/ppermute | solution.py:40
  13.0 15.0 %collective-permute-start.1 = (bf16[128,2048]{1,0:T(8,128)(2,1)}, bf16[128,2048]{1,0:T(8,128)(2,1)S(1)}, u32[]{:S(2)}, u32[]{:S(2)}) collective-permute-start(bf16[128,2048]{1,0:T(8,128)(2,1)} %get-tuple-element.21), channel_id=1, source_target_pairs={{0,16},{8,24},{16,0},{24,8},{1,17},{9,25},{17,1},{25,9},{2,18},{10... | collective-permute-start | bytes 1572872 | tf_op jit(solution)/shard_map/ppermute | solution.py:40
  14.6 6.2 %copy-start.11 = (s32[4]{0:T(128)S(1)}, s32[4]{0:T(128)}, u32[]{:S(2)}) copy-start(s32[4]{0:T(128)} %constant.41.clone) | copy-start | bytes 52
  14.6 6.3 %copy-start.10 = (s32[7]{0:T(128)S(1)}, s32[7]{0:T(128)}, u32[]{:S(2)}) copy-start(s32[7]{0:T(128)} %named_ref.5) | copy-start | bytes 88
  14.6 23.8 %collective-permute-start.2 = (bf16[128,2048]{1,0:T(8,128)(2,1)}, bf16[128,2048]{1,0:T(8,128)(2,1)S(1)}, u32[]{:S(2)}, u32[]{:S(2)}) collective-permute-start(bf16[128,2048]{1,0:T(8,128)(2,1)} %get-tuple-element.22), channel_id=1, source_target_pairs={{0,24},{8,16},{16,8},{24,0},{1,25},{9,17},{17,9},{25,1},{2,26},{10... | collective-permute-start | bytes 1572872 | tf_op jit(solution)/shard_map/ppermute | solution.py:40
  17.8 28.0 %collective-permute-start.3 = (bf16[128,2048]{1,0:T(8,128)(2,1)}, bf16[128,2048]{1,0:T(8,128)(2,1)S(1)}, u32[]{:S(2)}, u32[]{:S(2)}) collective-permute-start(bf16[128,2048]{1,0:T(8,128)(2,1)} %get-tuple-element.23), channel_id=1, source_target_pairs={{0,1},{1,0},{2,3},{3,2},{4,5},{5,4},{6,7},{7,6},{8,9},{9,8},{10,11... | collective-permute-start | bytes 1572872 | tf_op jit(solution)/shard_map/ppermute | solution.py:40
  19.4 40.1 %collective-permute-start.4 = (bf16[128,2048]{1,0:T(8,128)(2,1)}, bf16[128,2048]{1,0:T(8,128)(2,1)S(1)}, u32[]{:S(2)}, u32[]{:S(2)}) collective-permute-start(bf16[128,2048]{1,0:T(8,128)(2,1)} %get-tuple-element.24), channel_id=1, source_target_pairs={{0,3},{1,2},{2,1},{3,0},{4,7},{5,6},{6,5},{7,4},{8,11},{9,10},{10,... | collective-permute-start | bytes 1572872 | tf_op jit(solution)/shard_map/ppermute | solution.py:40
  21.7 16.7 %copy-start.3 = (bf16[128,2048]{1,0:T(8,128)(2,1)}, bf16[128,2048]{1,0:T(8,128)(2,1)S(1)}, u32[]{:S(2)}) copy-start(bf16[128,2048]{1,0:T(8,128)(2,1)S(1)} %collective-permute-done.rest_1_) | copy-start | bytes 1572868
  28.0 10.3 %copy-start.4 = (bf16[128,2048]{1,0:T(8,128)(2,1)}, bf16[128,2048]{1,0:T(8,128)(2,1)S(1)}, u32[]{:S(2)}) copy-start(bf16[128,2048]{1,0:T(8,128)(2,1)S(1)} %collective-permute-done.1.rest_2_) | copy-start | bytes 1572868
  43.6 33.2 %collective-permute-start.5 = (bf16[128,2048]{1,0:T(8,128)(2,1)}, bf16[128,2048]{1,0:T(8,128)(2,1)S(1)}, u32[]{:S(2)}, u32[]{:S(2)}) collective-permute-start(bf16[128,2048]{1,0:T(8,128)(2,1)} %get-tuple-element.27), channel_id=1, source_target_pairs={{0,8},{8,0},{16,24},{24,16},{1,9},{9,1},{17,25},{25,17},{2,10},{10... | collective-permute-start | bytes 1572872 | tf_op jit(solution)/shard_map/ppermute | solution.py:40
  44.3 32.5 %collective-permute-start.6 = (bf16[128,2048]{1,0:T(8,128)(2,1)}, bf16[128,2048]{1,0:T(8,128)(2,1)S(1)}, u32[]{:S(2)}, u32[]{:S(2)}) collective-permute-start(bf16[128,2048]{1,0:T(8,128)(2,1)} %get-tuple-element.28), channel_id=1, source_target_pairs={{0,16},{8,24},{16,0},{24,8},{1,17},{9,25},{17,1},{25,9},{2,18},{10... | collective-permute-start | bytes 1572872 | tf_op jit(solution)/shard_map/ppermute | solution.py:40
  45.8 31.0 %collective-permute-start.7 = (bf16[128,2048]{1,0:T(8,128)(2,1)}, bf16[128,2048]{1,0:T(8,128)(2,1)S(1)}, u32[]{:S(2)}, u32[]{:S(2)}) collective-permute-start(bf16[128,2048]{1,0:T(8,128)(2,1)} %get-tuple-element.29), channel_id=1, source_target_pairs={{0,24},{8,16},{16,8},{24,0},{1,25},{9,17},{17,9},{25,1},{2,26},{10... | collective-permute-start | bytes 1572872 | tf_op jit(solution)/shard_map/ppermute | solution.py:40
  49.5 44.3 %collective-permute-start.10 = (bf16[128,2048]{1,0:T(8,128)(2,1)}, bf16[128,2048]{1,0:T(8,128)(2,1)}, u32[]{:S(2)}, u32[]{:S(2)}) collective-permute-start(bf16[128,2048]{1,0:T(8,128)(2,1)} %get-tuple-element.25.rest_6_), channel_id=1, source_target_pairs={{0,5},{1,4},{2,7},{3,6},{4,1},{5,0},{6,3},{7,2},{8,13},{9,12},{10,... | collective-permute-start | bytes 1572872 | tf_op jit(solution)/shard_map/ppermute | solution.py:40
  59.5 17.3 %copy-start.1 = (bf16[128,2048]{1,0:T(8,128)(2,1)S(1)}, bf16[128,2048]{1,0:T(8,128)(2,1)}, u32[]{:S(2)}) copy-start(bf16[128,2048]{1,0:T(8,128)(2,1)} %get-tuple-element.26.rest_0_) | copy-start | bytes 1572868
  59.5 54.7 %collective-permute-start.12 = (bf16[128,2048]{1,0:T(8,128)(2,1)}, bf16[128,2048]{1,0:T(8,128)(2,1)}, u32[]{:S(2)}, u32[]{:S(2)}) collective-permute-start(bf16[128,2048]{1,0:T(8,128)(2,1)} %get-tuple-element.33), channel_id=1, source_target_pairs={{0,7},{1,6},{2,5},{3,4},{4,3},{5,2},{6,1},{7,0},{8,15},{9,14},{10,... | collective-permute-start | bytes 1572872 | tf_op jit(solution)/shard_map/ppermute | solution.py:40
  80.3 8.7 %copy-start.2 = (bf16[512,2048]{1,0:T(8,128)(2,1)S(1)}, bf16[512,2048]{1,0:T(8,128)(2,1)}, u32[]{:S(2)}) copy-start(bf16[512,2048]{1,0:T(8,128)(2,1)} %refresh.1) | copy-start | bytes 6291460
  80.3 8.7 %copy-start.7 = (bf16[128,2048]{1,0:T(8,128)(2,1)S(1)}, bf16[128,2048]{1,0:T(8,128)(2,1)}, u32[]{:S(2)}) copy-start(bf16[128,2048]{1,0:T(8,128)(2,1)} %copy-done.6) | copy-start | bytes 1572868
  84.8 32.4 %all-to-all-start.1 = ((bf16[4,128,512]{2,1,0:T(8,128)(2,1)}), bf16[4,128,512]{2,1,0:T(8,128)(2,1)S(1)}, u32[]{:S(2)}, u32[]{:S(2)}) async-start(bf16[4,128,512]{2,1,0:T(8,128)(2,1)} %bitcast.28), calls=%async_computation.1 | async-start | bytes 1048576 | tf_op jit(solution)/shard_map/all_to_all | solution.py:243
  89.0 2.3 %copy-start.9 = (bf16[128,2048]{1,0:T(8,128)(2,1)S(1)}, bf16[128,2048]{1,0:T(8,128)(2,1)}, u32[]{:S(2)}) copy-start(bf16[128,2048]{1,0:T(8,128)(2,1)} %copy-done.8) | copy-start | bytes 1572868
  89.8 27.4 %collective-permute-start.8 = (bf16[128,512]{1,0:T(8,128)(2,1)S(1)}, bf16[128,512]{1,0:T(8,128)(2,1)S(1)}, u32[]{:S(2)}, u32[]{:S(2)}) collective-permute-start(bf16[128,512]{1,0:T(8,128)(2,1)S(1)} %convolution_convert_fusion.4), channel_id=1, source_target_pairs={{1,0},{0,1},{3,2},{2,3},{5,4},{4,5},{7,6},{6,7},{9,8},{8,9},{11,10... | collective-permute-start | bytes 393224 | tf_op jit(solution)/shard_map/ppermute | solution.py:44
  92.1 25.2 %collective-permute-start.9 = (bf16[128,512]{1,0:T(8,128)(2,1)S(1)}, bf16[128,512]{1,0:T(8,128)(2,1)S(1)}, u32[]{:S(2)}, u32[]{:S(2)}) collective-permute-start(bf16[128,512]{1,0:T(8,128)(2,1)S(1)} %convolution_convert_fusion.3), channel_id=1, source_target_pairs={{3,0},{2,1},{1,2},{0,3},{7,4},{6,5},{5,6},{4,7},{11,8},{10,9},{9,1... | collective-permute-start | bytes 393224 | tf_op jit(solution)/shard_map/ppermute | solution.py:44
  95.6 24.3 %collective-permute-start.11 = (bf16[128,512]{1,0:T(8,128)(2,1)S(1)}, bf16[128,512]{1,0:T(8,128)(2,1)S(1)}, u32[]{:S(2)}, u32[]{:S(2)}) collective-permute-start(bf16[128,512]{1,0:T(8,128)(2,1)S(1)} %convolution_convert_fusion.2), channel_id=1, source_target_pairs={{5,0},{4,1},{7,2},{6,3},{1,4},{0,5},{3,6},{2,7},{13,8},{12,9},{15,... | collective-permute-start | bytes 393224 | tf_op jit(solution)/shard_map/ppermute | solution.py:44
  116.1 7.8 %collective-permute-start.13 = (bf16[128,512]{1,0:T(8,128)(2,1)S(1)}, bf16[128,512]{1,0:T(8,128)(2,1)S(1)}, u32[]{:S(2)}, u32[]{:S(2)}) collective-permute-start(bf16[128,512]{1,0:T(8,128)(2,1)S(1)} %convolution_convert_fusion.1), channel_id=1, source_target_pairs={{7,0},{6,1},{5,2},{4,3},{3,4},{2,5},{1,6},{0,7},{15,8},{14,9},{13,... | collective-permute-start | bytes 393224 | tf_op jit(solution)/shard_map/ppermute | solution.py:44
  (4 other events, 4.0 us)

commit v4 on v3

--- a/solution.py
+++ b/solution.py
@@ -56,15 +56,21 @@
 
 
 def pick_kernel(wanted, owners, tokens_ref, named_ref, *rest):
-    outs, sem = rest[-1 - len(wanted) : -1], rest[-1]
-    if rest[-2].ndim == 3:
-        outs = [rest[-2].at[k] for k in range(len(wanted))]
+    held, sem, sent = rest[-3:]
+    outs = rest[-3 - len(wanted) : -3]
+    if len(rest[-4].shape) == 3:
+        outs = [rest[-4].at[k] for k in range(len(wanted))]
     copies = []
     for k, group_of in enumerate(wanted):
         slot = block_of(group_of(), named_ref, tokens_ref.shape[0], owners)
-        copies.append(pltpu.make_async_copy(tokens_ref.at[slot], outs[k], sem.at[k]))
+        copies.append(pltpu.make_async_copy(tokens_ref.at[slot], held.at[k], sem.at[k]))
         copies[-1].start()
-    for copy in copies:
+    leaving = []
+    for k, copy in enumerate(copies):
+        copy.wait()
+        leaving.append(pltpu.make_async_copy(held.at[k], outs[k], sent.at[k]))
+        leaving[-1].start()
+    for copy in leaving:
         copy.wait()
 
 
@@ -79,8 +85,9 @@
         functools.partial(pick_kernel, wanted, owners),
         out_shape=out_shape,
         in_specs=[ANY, SMEM] + [ANY] * len(later_than),
-        out_specs=VMEM if stacked else [VMEM] * len(wanted),
-        scratch_shapes=[pltpu.SemaphoreType.DMA((len(wanted),))],
+        out_specs=ANY if stacked else [ANY] * len(wanted),
+        scratch_shapes=[pltpu.VMEM((len(wanted),) + shape, resident.dtype)]
+        + [pltpu.SemaphoreType.DMA((len(wanted),))] * 2,
         compiler_params=pltpu.CompilerParams(vmem_limit_bytes=56 << 20),
         cost_estimate=pl.CostEstimate(flops=0, bytes_accessed=2 * size, transcendentals=0),
         name="pick",

time: 128 us -> 127 us (level)
  transfers between devices with their start and end apart: 16 -> 16, of which waited for: 7 -> 7; matrix products, arithmetic and copies ran while one was open for 9% -> 9% of each run, Pallas kernels for 26% -> 25%
where the time goes in v4:
time: 127 us; the launch traced here: 125 us
  waiting for transfers between devices  48.4 us (38%)
  Pallas kernels  34.9 us (27%)
  starting transfers between devices  24.6 us (19%)
  matrix products  9.87 us (8%)
  local copies, waits for them, and re-layouts  5.65 us (4%)
    ppermute x10, waiting for transfers between devices, send(): lax.ppermute(value, axis, [(i, partner(i, step, size)) for i in range(siz...  41.5 us
    pallas_call x1, Pallas kernels, orthogonalize(): pl.pallas_call(functools.partial(newton_kernel, chunk, owners), out_shape...  16.4 us
    dot_general x5, matrix products, product(): lax.dot_general(block, refreshed, ROW_BY_ROW, preferred_element_type=jnp....  9.87 us
    all_to_all x2, starting transfers between devices, exchange(): lax.all_to_all(blocks, 'replica', 0, 0, axis_index_groups=teams, tiled=True)  9.41 us
    pallas_call x3, Pallas kernels, pick(): pl.pallas_call(functools.partial(pick_kernel, wanted, owners), out_shape=...  8.56 us
    ppermute x10, starting transfers between devices, send(): lax.ppermute(value, axis, [(i, partner(i, step, size)) for i in range(siz...  8.18 us
    pallas_call x2, Pallas kernels, by_owner(): pl.pallas_call(functools.partial(by_owner_kernel, owners, scale, len(late...  7.92 us
    ppermute x4, starting transfers between devices, send_back(): lax.ppermute(value, axis, [(partner(i, step, size), i) for i in range(siz...  6.98 us
  transfers between devices with their start and end apart: 16, of which 7 were waited for; matrix products, arithmetic and copies ran while one was open for 9% of the time, Pallas kernels for 25%

profile of v4, /device:TPU:16, one launch (start us, length us, event | category | flops | bytes accessed | tf_op | source)
XLA Modules:
  0.0 125.0 jit_solution(8228063495204560100)
XLA Ops:
  0.6 3.1 %pick.3.rest_0_ = bf16[4,128,2048]{2,1,0:T(8,128)(2,1)} custom-call(bf16[7,128,2048]{2,1,0:T(8,128)(2,1)} %bitcast.24, s32[7]{0:T(128)} %named_ref.5), custom_call_target="tpu_custom_call" | custom-call | bytes 4194304 | tf_op jit(solution)/shard_map/pick/pallas_call | solution.py:84
  3.7 5.2 %all-to-all-start = ((bf16[4,128,2048]{2,1,0:T(8,128)(2,1)}), bf16[4,128,2048]{2,1,0:T(8,128)(2,1)}, u32[]{:S(2)}, u32[]{:S(2)}) async-start(bf16[4,128,2048]{2,1,0:T(8,128)(2,1)} %pick.3.rest_0_), calls=%async_computation | async-start | bytes 4194304 | tf_op jit(solution)/shard_map/all_to_all | solution.py:250
  9.0 3.6 %by_owner.2 = (bf16[128,2048]{1,0:T(8,128)(2,1)}, bf16[128,2048]{1,0:T(8,128)(2,1)}, bf16[128,2048]{1,0:T(8,128)(2,1)}, bf16[128,2048]{1,0:T(8,128)(2,1)}) custom-call(bf16[4,128,2048]{2,1,0:T(8,128)(2,1)} %array_ref.2, s32[32]{0:T(128)} %owner_ref.3, bf16[4,128,2048]{2,1,0:T(8,128)(2,1)} %pick.3.rest_0_), custom_call_target="tpu_custom_call" | custom-call | bytes 4194304 | tf_op jit(solution)/shard_map/by_owner/pallas_call | solution.py:120
  12.6 1.6 %collective-permute-start.1 = (bf16[128,2048]{1,0:T(8,128)(2,1)}, bf16[128,2048]{1,0:T(8,128)(2,1)S(1)}, u32[]{:S(2)}, u32[]{:S(2)}) collective-permute-start(bf16[128,2048]{1,0:T(8,128)(2,1)} %get-tuple-element.21), channel_id=1, source_target_pairs={{0,16},{8,24},{16,0},{24,8},{1,17},{9,25},{17,1},{25,9},{2,18},{10... | collective-permute-start | bytes 1572872 | tf_op jit(solution)/shard_map/ppermute | solution.py:40
  14.5 2.7 %pick.4 = (bf16[128,2048]{1,0:T(8,128)(2,1)}, bf16[128,2048]{1,0:T(8,128)(2,1)}) custom-call(bf16[7,128,2048]{2,1,0:T(8,128)(2,1)} %bitcast.25, s32[7]{0:T(128)} %named_ref.5, bf16[4,128,2048]{2,1,0:T(8,128)(2,1)} %pick.3.rest_0_), custom_call_target="tpu_custom_call" | custom-call | bytes 2097152 | tf_op jit(solution)/shard_map/pick/pallas_call | solution.py:84
  17.2 1.6 %collective-permute-start.3 = (bf16[128,2048]{1,0:T(8,128)(2,1)}, bf16[128,2048]{1,0:T(8,128)(2,1)S(1)}, u32[]{:S(2)}, u32[]{:S(2)}) collective-permute-start(bf16[128,2048]{1,0:T(8,128)(2,1)} %get-tuple-element.23), channel_id=1, source_target_pairs={{0,1},{1,0},{2,3},{3,2},{4,5},{5,4},{6,7},{7,6},{8,9},{9,8},{10,11... | collective-permute-start | bytes 1572872 | tf_op jit(solution)/shard_map/ppermute | solution.py:40
  21.1 6.5 %collective-permute-done.1.rest_2_ = bf16[128,2048]{1,0:T(8,128)(2,1)S(1)} collective-permute-done((bf16[128,2048]{1,0:T(8,128)(2,1)}, bf16[128,2048]{1,0:T(8,128)(2,1)S(1)}, u32[]{:S(2)}, u32[]{:S(2)}) %collective-permute-start.1) | collective-permute-done | bytes 524320 | tf_op jit(solution)/shard_map/ppermute | solution.py:40
  27.6 10.3 %collective-permute-done.2.rest_3_ = bf16[128,2048]{1,0:T(8,128)(2,1)S(1)} collective-permute-done((bf16[128,2048]{1,0:T(8,128)(2,1)}, bf16[128,2048]{1,0:T(8,128)(2,1)S(1)}, u32[]{:S(2)}, u32[]{:S(2)}) %collective-permute-start.2) | collective-permute-done | bytes 524320 | tf_op jit(solution)/shard_map/ppermute | solution.py:40
  38.8 4.4 %by_owner.3 = (bf16[128,2048]{1,0:T(8,128)(2,1)}, bf16[128,2048]{1,0:T(8,128)(2,1)}, bf16[128,2048]{1,0:T(8,128)(2,1)}, bf16[128,2048]{1,0:T(8,128)(2,1)}) custom-call(f32[4,128,2048]{2,1,0:T(8,128)} %array_ref.3, s32[32]{0:T(128)} %owner_ref.3, bf16[128,2048]{1,0:T(8,128)(2,1)} %get-tuple-element.19.rest_0_, bf16[128,2048]{1,0:T(8,128)(2,1)} %copy-done.3, ...), custom_call_target="tpu_custom_call" | custom-call | bytes 6291456 | tf_op jit(solution)/shard_map/by_owner/pallas_call | solution.py:120
  46.2 2.7 %pick.5 = (bf16[128,2048]{1,0:T(8,128)(2,1)}, bf16[128,2048]{1,0:T(8,128)(2,1)}) custom-call(bf16[7,128,2048]{2,1,0:T(8,128)(2,1)} %bitcast.26, s32[7]{0:T(128)} %named_ref.5, bf16[128,2048]{1,0:T(8,128)(2,1)} %get-tuple-element.19.rest_0_, bf16[128,2048]{1,0:T(8,128)(2,1)} %copy-done.3, bf16[128,2048]{1,0:T(8,128)(2,1)} %copy-done.4, ...), custom_call_target="tpu_custom_call" | custom-call | bytes 2097152 | tf_op jit(solution)/shard_map/pick/pallas_call | solution.py:84
  49.9 9.2 %collective-permute-done.4.rest_5_ = bf16[128,2048]{1,0:T(8,128)(2,1)S(1)} collective-permute-done((bf16[128,2048]{1,0:T(8,128)(2,1)}, bf16[128,2048]{1,0:T(8,128)(2,1)S(1)}, u32[]{:S(2)}, u32[]{:S(2)}) %collective-permute-start.4) | collective-permute-done | bytes 524320 | tf_op jit(solution)/shard_map/ppermute | solution.py:40
  59.9 16.4 %newton.1.update_ref = bf16[512,2048]{1,0:T(8,128)(2,1)} custom-call(bf16[128,2048]{1,0:T(8,128)(2,1)} %get-tuple-element.19.rest_0_, bf16[128,2048]{1,0:T(8,128)(2,1)} %copy-done.3, bf16[128,2048]{1,0:T(8,128)(2,1)} %copy-done.4, bf16[128,2048]{1,0:T(8,128)(2,1)} %copy-done.5, bf16[128,2048]{1,0:T(8,128)(2,1)} %copy-done.6, bf16[128,2048]{1,0:T(8,128)(2,1)} %copy-done.8, ...), custom_call_target="tpu_custom_call" | custom-call | flops 9663676416 | bytes 4194304 | tf_op jit(solution)/shard_map/newton/pallas_call | solution.py:177
  76.4 1.6 %copy-done = bf16[512,2048]{1,0:T(8,128)(2,1)S(1)} copy-done((bf16[512,2048]{1,0:T(8,128)(2,1)S(1)}, bf16[512,2048]{1,0:T(8,128)(2,1)}, u32[]{:S(2)}) %copy-start) | copy-done | bytes 2097176
  78.0 1.9 %refresh.1 = bf16[512,2048]{1,0:T(8,128)(2,1)} custom-call(bf16[512,2048]{1,0:T(8,128)(2,1)S(1)} %copy-done, bf16[128,2048]{1,0:T(8,128)(2,1)S(1)} %copy-done.1, bf16[128,2048]{1,0:T(8,128)(2,1)S(1)} %collective-permute-done.5.rest_1_, bf16[128,2048]{1,0:T(8,128)(2,1)S(1)} %collective-permute-done.6.rest_2_, bf16[128,2048]{1,0:T(8,128)(2,1)S(1)} %collective-permute-done.7.rest_3_), custom_call_target="tpu_custom_call" | custom-call | flops 2097152 | bytes 6291456 | tf_op jit(solution)/shard_map/refresh/pallas_call | solution.py:206
  79.9 4.5 %convolution_convert_fusion = bf16[512,512]{1,0:T(8,128)(2,1)} fusion(bf16[512,2048]{1,0:T(8,128)(2,1)} %bitcast.2, bf16[512,2048]{1,0:T(8,128)(2,1)} %refresh.1), kind=kOutput, calls=%fused_computation.1 | convolution fusion | flops 1074003968 | bytes 4718592 | tf_op jit(solution)/shard_map/dot_general | solution.py:265
  84.4 4.2 %all-to-all-start.1 = ((bf16[4,128,512]{2,1,0:T(8,128)(2,1)}), bf16[4,128,512]{2,1,0:T(8,128)(2,1)S(1)}, u32[]{:S(2)}, u32[]{:S(2)}) async-start(bf16[4,128,512]{2,1,0:T(8,128)(2,1)} %bitcast.28), calls=%async_computation.1 | async-start | bytes 1048576 | tf_op jit(solution)/shard_map/all_to_all | solution.py:250
  91.7 1.6 %collective-permute-start.9 = (bf16[128,512]{1,0:T(8,128)(2,1)S(1)}, bf16[128,512]{1,0:T(8,128)(2,1)S(1)}, u32[]{:S(2)}, u32[]{:S(2)}) collective-permute-start(bf16[128,512]{1,0:T(8,128)(2,1)S(1)} %convolution_convert_fusion.3), channel_id=1, source_target_pairs={{3,0},{2,1},{1,2},{0,3},{7,4},{6,5},{5,6},{4,7},{11,8},{10,9},{9,1... | collective-permute-start | bytes 393224 | tf_op jit(solution)/shard_map/ppermute | solution.py:44
  93.3 1.9 %convolution_convert_fusion.2 = bf16[128,512]{1,0:T(8,128)(2,1)S(1)} fusion(bf16[128,2048]{1,0:T(8,128)(2,1)} %collective-permute-done.10, bf16[512,2048]{1,0:T(8,128)(2,1)S(1)} %copy-done.2), kind=kOutput, calls=%fused_computation.3 | convolution fusion | flops 268500992 | bytes 2752512 | tf_op jit(solution)/shard_map/dot_general | solution.py:265
  95.2 3.1 %collective-permute-start.11 = (bf16[128,512]{1,0:T(8,128)(2,1)S(1)}, bf16[128,512]{1,0:T(8,128)(2,1)S(1)}, u32[]{:S(2)}, u32[]{:S(2)}) collective-permute-start(bf16[128,512]{1,0:T(8,128)(2,1)S(1)} %convolution_convert_fusion.2), channel_id=1, source_target_pairs={{5,0},{4,1},{7,2},{6,3},{1,4},{0,5},{3,6},{2,7},{13,8},{12,9},{15,... | collective-permute-start | bytes 393224 | tf_op jit(solution)/shard_map/ppermute | solution.py:44
  98.3 15.5 %collective-permute-done.12 = bf16[128,2048]{1,0:T(8,128)(2,1)} collective-permute-done((bf16[128,2048]{1,0:T(8,128)(2,1)}, bf16[128,2048]{1,0:T(8,128)(2,1)}, u32[]{:S(2)}, u32[]{:S(2)}) %collective-permute-start.12) | collective-permute-done | bytes 524320 | tf_op jit(solution)/shard_map/ppermute | solution.py:40
  113.8 1.9 %convolution_convert_fusion.1 = bf16[128,512]{1,0:T(8,128)(2,1)S(1)} fusion(bf16[128,2048]{1,0:T(8,128)(2,1)} %collective-permute-done.12, bf16[512,2048]{1,0:T(8,128)(2,1)S(1)} %copy-done.2), kind=kOutput, calls=%fused_computation.2 | convolution fusion | flops 268500992 | bytes 2752512 | tf_op jit(solution)/shard_map/dot_general | solution.py:265
  116.9 2.6 %collective-permute-done.11 = bf16[128,512]{1,0:T(8,128)(2,1)S(1)} collective-permute-done((bf16[128,512]{1,0:T(8,128)(2,1)S(1)}, bf16[128,512]{1,0:T(8,128)(2,1)S(1)}, u32[]{:S(2)}, u32[]{:S(2)}) %collective-permute-start.11) | collective-permute-done | bytes 131104 | tf_op jit(solution)/shard_map/ppermute | solution.py:44
  119.5 4.0 %collective-permute-done.13 = bf16[128,512]{1,0:T(8,128)(2,1)S(1)} collective-permute-done((bf16[128,512]{1,0:T(8,128)(2,1)S(1)}, bf16[128,512]{1,0:T(8,128)(2,1)S(1)}, u32[]{:S(2)}, u32[]{:S(2)}) %collective-permute-start.13) | collective-permute-done | bytes 131104 | tf_op jit(solution)/shard_map/ppermute | solution.py:44
  123.5 1.5 %gather_fusion = bf16[7,128,512]{2,1,0:T(8,128)(2,1)} fusion(bf16[8,128,512]{2,1,0:T(8,128)(2,1)S(1)} %bitcast_dynamic-update-slice_fusion, s32[1024]{0:T(1024)S(1)} %pad_clamp_fusion), kind=kCustom, calls=%fused_computation | custom fusion | bytes 1835036 | tf_op jit(solution)/shard_map/jit(_take)/gather | solution.py:283
  (55 shorter events, 12.7 us)
Async XLA Ops:
  3.7 76.1 %all-to-all-start = ((bf16[4,128,2048]{2,1,0:T(8,128)(2,1)}), bf16[4,128,2048]{2,1,0:T(8,128)(2,1)}, u32[]{:S(2)}, u32[]{:S(2)}) async-start(bf16[4,128,2048]{2,1,0:T(8,128)(2,1)} %pick.3.rest_0_), calls=%async_computation | async-start | bytes 4194304 | tf_op jit(solution)/shard_map/all_to_all | solution.py:250
  12.5 8.6 %collective-permute-start = (bf16[128,2048]{1,0:T(8,128)(2,1)}, bf16[128,2048]{1,0:T(8,128)(2,1)S(1)}, u32[]{:S(2)}, u32[]{:S(2)}) collective-permute-start(bf16[128,2048]{1,0:T(8,128)(2,1)} %get-tuple-element.20), channel_id=1, source_target_pairs={{0,8},{8,0},{16,24},{24,16},{1,9},{9,1},{17,25},{25,17},{2,10},{10... | collective-permute-start | bytes 1572872 | tf_op jit(solution)/shard_map/ppermute | solution.py:40
  12.6 15.0 %collective-permute-start.1 = (bf16[128,2048]{1,0:T(8,128)(2,1)}, bf16[128,2048]{1,0:T(8,128)(2,1)S(1)}, u32[]{:S(2)}, u32[]{:S(2)}) collective-permute-start(bf16[128,2048]{1,0:T(8,128)(2,1)} %get-tuple-element.21), channel_id=1, source_target_pairs={{0,16},{8,24},{16,0},{24,8},{1,17},{9,25},{17,1},{25,9},{2,18},{10... | collective-permute-start | bytes 1572872 | tf_op jit(solution)/shard_map/ppermute | solution.py:40
  14.2 6.0 %copy-start.11 = (s32[4]{0:T(128)S(1)}, s32[4]{0:T(128)}, u32[]{:S(2)}) copy-start(s32[4]{0:T(128)} %constant.41.clone) | copy-start | bytes 52
  14.2 6.1 %copy-start.10 = (s32[7]{0:T(128)S(1)}, s32[7]{0:T(128)}, u32[]{:S(2)}) copy-start(s32[7]{0:T(128)} %named_ref.5) | copy-start | bytes 88
  14.2 23.8 %collective-permute-start.2 = (bf16[128,2048]{1,0:T(8,128)(2,1)}, bf16[128,2048]{1,0:T(8,128)(2,1)S(1)}, u32[]{:S(2)}, u32[]{:S(2)}) collective-permute-start(bf16[128,2048]{1,0:T(8,128)(2,1)} %get-tuple-element.22), channel_id=1, source_target_pairs={{0,24},{8,16},{16,8},{24,0},{1,25},{9,17},{17,9},{25,1},{2,26},{10... | collective-permute-start | bytes 1572872 | tf_op jit(solution)/shard_map/ppermute | solution.py:40
  17.2 28.2 %collective-permute-start.3 = (bf16[128,2048]{1,0:T(8,128)(2,1)}, bf16[128,2048]{1,0:T(8,128)(2,1)S(1)}, u32[]{:S(2)}, u32[]{:S(2)}) collective-permute-start(bf16[128,2048]{1,0:T(8,128)(2,1)} %get-tuple-element.23), channel_id=1, source_target_pairs={{0,1},{1,0},{2,3},{3,2},{4,5},{5,4},{6,7},{7,6},{8,9},{9,8},{10,11... | collective-permute-start | bytes 1572872 | tf_op jit(solution)/shard_map/ppermute | solution.py:40
  18.8 40.3 %collective-permute-start.4 = (bf16[128,2048]{1,0:T(8,128)(2,1)}, bf16[128,2048]{1,0:T(8,128)(2,1)S(1)}, u32[]{:S(2)}, u32[]{:S(2)}) collective-permute-start(bf16[128,2048]{1,0:T(8,128)(2,1)} %get-tuple-element.24), channel_id=1, source_target_pairs={{0,3},{1,2},{2,1},{3,0},{4,7},{5,6},{6,5},{7,4},{8,11},{9,10},{10,... | collective-permute-start | bytes 1572872 | tf_op jit(solution)/shard_map/ppermute | solution.py:40
  21.1 16.9 %copy-start.3 = (bf16[128,2048]{1,0:T(8,128)(2,1)}, bf16[128,2048]{1,0:T(8,128)(2,1)S(1)}, u32[]{:S(2)}) copy-start(bf16[128,2048]{1,0:T(8,128)(2,1)S(1)} %collective-permute-done.rest_1_) | copy-start | bytes 1572868
  27.6 10.3 %copy-start.4 = (bf16[128,2048]{1,0:T(8,128)(2,1)}, bf16[128,2048]{1,0:T(8,128)(2,1)S(1)}, u32[]{:S(2)}) copy-start(bf16[128,2048]{1,0:T(8,128)(2,1)S(1)} %collective-permute-done.1.rest_2_) | copy-start | bytes 1572868
  43.1 33.2 %collective-permute-start.5 = (bf16[128,2048]{1,0:T(8,128)(2,1)}, bf16[128,2048]{1,0:T(8,128)(2,1)S(1)}, u32[]{:S(2)}, u32[]{:S(2)}) collective-permute-start(bf16[128,2048]{1,0:T(8,128)(2,1)} %get-tuple-element.27), channel_id=1, source_target_pairs={{0,8},{8,0},{16,24},{24,16},{1,9},{9,1},{17,25},{25,17},{2,10},{10... | collective-permute-start | bytes 1572872 | tf_op jit(solution)/shard_map/ppermute | solution.py:40
  43.9 32.5 %collective-permute-start.6 = (bf16[128,2048]{1,0:T(8,128)(2,1)}, bf16[128,2048]{1,0:T(8,128)(2,1)S(1)}, u32[]{:S(2)}, u32[]{:S(2)}) collective-permute-start(bf16[128,2048]{1,0:T(8,128)(2,1)} %get-tuple-element.28), channel_id=1, source_target_pairs={{0,16},{8,24},{16,0},{24,8},{1,17},{9,25},{17,1},{25,9},{2,18},{10... | collective-permute-start | bytes 1572872 | tf_op jit(solution)/shard_map/ppermute | solution.py:40
  45.4 31.0 %collective-permute-start.7 = (bf16[128,2048]{1,0:T(8,128)(2,1)}, bf16[128,2048]{1,0:T(8,128)(2,1)S(1)}, u32[]{:S(2)}, u32[]{:S(2)}) collective-permute-start(bf16[128,2048]{1,0:T(8,128)(2,1)} %get-tuple-element.29), channel_id=1, source_target_pairs={{0,24},{8,16},{16,8},{24,0},{1,25},{9,17},{17,9},{25,1},{2,26},{10... | collective-permute-start | bytes 1572872 | tf_op jit(solution)/shard_map/ppermute | solution.py:40
  48.9 44.4 %collective-permute-start.10 = (bf16[128,2048]{1,0:T(8,128)(2,1)}, bf16[128,2048]{1,0:T(8,128)(2,1)}, u32[]{:S(2)}, u32[]{:S(2)}) collective-permute-start(bf16[128,2048]{1,0:T(8,128)(2,1)} %get-tuple-element.25.rest_6_), channel_id=1, source_target_pairs={{0,5},{1,4},{2,7},{3,6},{4,1},{5,0},{6,3},{7,2},{8,13},{9,12},{10,... | collective-permute-start | bytes 1572872 | tf_op jit(solution)/shard_map/ppermute | solution.py:40
  59.1 17.3 %copy-start.1 = (bf16[128,2048]{1,0:T(8,128)(2,1)S(1)}, bf16[128,2048]{1,0:T(8,128)(2,1)}, u32[]{:S(2)}) copy-start(bf16[128,2048]{1,0:T(8,128)(2,1)} %get-tuple-element.26.rest_0_) | copy-start | bytes 1572868
  59.1 54.7 %collective-permute-start.12 = (bf16[128,2048]{1,0:T(8,128)(2,1)}, bf16[128,2048]{1,0:T(8,128)(2,1)}, u32[]{:S(2)}, u32[]{:S(2)}) collective-permute-start(bf16[128,2048]{1,0:T(8,128)(2,1)} %get-tuple-element.33), channel_id=1, source_target_pairs={{0,7},{1,6},{2,5},{3,4},{4,3},{5,2},{6,1},{7,0},{8,15},{9,14},{10,... | collective-permute-start | bytes 1572872 | tf_op jit(solution)/shard_map/ppermute | solution.py:40
  79.9 8.7 %copy-start.2 = (bf16[512,2048]{1,0:T(8,128)(2,1)S(1)}, bf16[512,2048]{1,0:T(8,128)(2,1)}, u32[]{:S(2)}) copy-start(bf16[512,2048]{1,0:T(8,128)(2,1)} %refresh.1) | copy-start | bytes 6291460
  79.9 8.7 %copy-start.7 = (bf16[128,2048]{1,0:T(8,128)(2,1)S(1)}, bf16[128,2048]{1,0:T(8,128)(2,1)}, u32[]{:S(2)}) copy-start(bf16[128,2048]{1,0:T(8,128)(2,1)} %copy-done.6) | copy-start | bytes 1572868
  84.4 32.4 %all-to-all-start.1 = ((bf16[4,128,512]{2,1,0:T(8,128)(2,1)}), bf16[4,128,512]{2,1,0:T(8,128)(2,1)S(1)}, u32[]{:S(2)}, u32[]{:S(2)}) async-start(bf16[4,128,512]{2,1,0:T(8,128)(2,1)} %bitcast.28), calls=%async_computation.1 | async-start | bytes 1048576 | tf_op jit(solution)/shard_map/all_to_all | solution.py:250
  88.6 2.3 %copy-start.9 = (bf16[128,2048]{1,0:T(8,128)(2,1)S(1)}, bf16[128,2048]{1,0:T(8,128)(2,1)}, u32[]{:S(2)}) copy-start(bf16[128,2048]{1,0:T(8,128)(2,1)} %copy-done.8) | copy-start | bytes 1572868
  89.4 27.4 %collective-permute-start.8 = (bf16[128,512]{1,0:T(8,128)(2,1)S(1)}, bf16[128,512]{1,0:T(8,128)(2,1)S(1)}, u32[]{:S(2)}, u32[]{:S(2)}) collective-permute-start(bf16[128,512]{1,0:T(8,128)(2,1)S(1)} %convolution_convert_fusion.4), channel_id=1, source_target_pairs={{1,0},{0,1},{3,2},{2,3},{5,4},{4,5},{7,6},{6,7},{9,8},{8,9},{11,10... | collective-permute-start | bytes 393224 | tf_op jit(solution)/shard_map/ppermute | solution.py:44
  91.7 25.2 %collective-permute-start.9 = (bf16[128,512]{1,0:T(8,128)(2,1)S(1)}, bf16[128,512]{1,0:T(8,128)(2,1)S(1)}, u32[]{:S(2)}, u32[]{:S(2)}) collective-permute-start(bf16[128,512]{1,0:T(8,128)(2,1)S(1)} %convolution_convert_fusion.3), channel_id=1, source_target_pairs={{3,0},{2,1},{1,2},{0,3},{7,4},{6,5},{5,6},{4,7},{11,8},{10,9},{9,1... | collective-permute-start | bytes 393224 | tf_op jit(solution)/shard_map/ppermute | solution.py:44
  95.2 24.3 %collective-permute-start.11 = (bf16[128,512]{1,0:T(8,128)(2,1)S(1)}, bf16[128,512]{1,0:T(8,128)(2,1)S(1)}, u32[]{:S(2)}, u32[]{:S(2)}) collective-permute-start(bf16[128,512]{1,0:T(8,128)(2,1)S(1)} %convolution_convert_fusion.2), channel_id=1, source_target_pairs={{5,0},{4,1},{7,2},{6,3},{1,4},{0,5},{3,6},{2,7},{13,8},{12,9},{15,... | collective-permute-start | bytes 393224 | tf_op jit(solution)/shard_map/ppermute | solution.py:44
  115.7 7.8 %collective-permute-start.13 = (bf16[128,512]{1,0:T(8,128)(2,1)S(1)}, bf16[128,512]{1,0:T(8,128)(2,1)S(1)}, u32[]{:S(2)}, u32[]{:S(2)}) collective-permute-start(bf16[128,512]{1,0:T(8,128)(2,1)S(1)} %convolution_convert_fusion.1), channel_id=1, source_target_pairs={{7,0},{6,1},{5,2},{4,3},{3,4},{2,5},{1,6},{0,7},{15,8},{14,9},{13,... | collective-permute-start | bytes 393224 | tf_op jit(solution)/shard_map/ppermute | solution.py:44
  (4 other events, 4.0 us)
